TPU v7x, 128 devices: a whole 4x4x4 slice. The times are simulated.
128 devices in a mesh: tm: 32 (over z, y_hi, x), space: 4 (over y_lo, core).
Axes of the slice: x: 4, y: 4 (y_hi: 2, y_lo: 2; y = y_hi * 2 + y_lo), z: 4, core: 2. Of those that a mesh axis runs over, the one named last changes fastest.
Arguments:
- initial_field: float32 [48, 2048], P(None, 'space'), may hold values from -6 to 6
- decay_rates: float32 [48, 2048], P(None, 'space'), may hold values from 0.001 to 1
- source: float32 [48, 2048], P(None, 'space'), may hold values from -5 to 5
- diffusion: float32 [48], replicated, may hold values from 0.02 to 0.5
- saturation: float32 [48], replicated, may hold values from 0.1 to 1
- conversion: float32 [48, 48], replicated, may hold values from 0.01 to 0.5
Outputs:
- coarse_points: float32 [32, 48, 2048], P('tm', None, 'space')
All inputs are finite; a program needn't handle non-finite values.
Results may differ from a plain program's by a relative error of at most 0.0003.
Values may be sent and summed in bfloat16 or wider, within the bound.
No kernel may reach another device: no remote copies, remote signals or barrier semaphores. Data moves between devices by JAX's collectives and lax.ppermute only.
A program may use at most 128 MiB of HBM per device.

v0:
```python
import jax
import jax.numpy as jnp
from jax import lax
from jax.sharding import PartitionSpec as P

COLS = 128
FACTOR = 4
NEWTON = 2
CYCLES = 2


precise = lax.Precision.HIGHEST


def extended(shard, sides, width):
    for axis, dim in sides:
        size, length = (lax.axis_size(axis), shard.shape[dim])
        up = [(i, (i + 1) % size) for i in range(size - 1)]
        down = [(j, i) for i, j in up]
        last = lax.slice_in_dim(shard, length - width, length, axis=dim)
        initial = lax.slice_in_dim(shard, 0, width, axis=dim)
        before = lax.ppermute(last, axis, up)
        after = lax.ppermute(initial, axis, down)
        shard = jnp.concatenate([before, shard, after], axis=dim)
    return shard


def passed_along(block, axis, distance):
    devices = range(lax.axis_size(axis))
    route = [(i - distance, i) for i in devices if i - distance in devices]
    return lax.ppermute(block, axis, route)


def conversion_parts(conversion):
    species = conversion.shape[0]
    identity = jnp.eye(species, dtype=jnp.float32)
    off_diagonal = conversion * (1.0 - identity)
    return (off_diagonal, jnp.sum(off_diagonal, axis=0))


def laplace(padded, columns, cell_count):
    middle = padded[:, columns : columns + cell_count]
    upper_row = padded[:, 0:cell_count]
    lower_row = padded[:, 2 * columns : 2 * columns + cell_count]
    left_side = padded[:, columns - 1 : columns - 1 + cell_count]
    right_side = padded[:, columns + 1 : columns + 1 + cell_count]
    position = jnp.arange(cell_count, dtype=jnp.int32) % columns
    left_side = jnp.where(position[None, :] != 0, left_side, 0.0)
    right_side = jnp.where(position[None, :] != columns - 1, right_side, 0.0)
    return upper_row + lower_row + left_side + right_side - 4.0 * middle


def tendency(padded, columns, decay_rates, source, diffusion, saturation, off_diagonal, outflow):
    cell_count = decay_rates.shape[1]
    field_now = padded[:, columns : columns + cell_count]
    spread = laplace(padded, columns, cell_count)
    mixing = jnp.dot(off_diagonal, field_now, precision=precise)
    squared = field_now * field_now
    saturated = squared * field_now / (1.0 + squared)
    return (
        diffusion[:, None] * spread
        + mixing
        - (outflow[:, None] + decay_rates) * field_now
        - saturation[:, None] * saturated
        + source
    )


def jacobian(step_length, decay_rates, diffusion, off_diagonal, outflow):
    species = off_diagonal.shape[0]
    diagonal = 1.0 + step_length * (4.0 * diffusion[:, None] + outflow[:, None] + decay_rates)
    identity = jnp.eye(species, dtype=jnp.float32)
    return identity[:, :, None] * diagonal[None, :, :] - step_length * off_diagonal[:, :, None]


def invert(matrices):
    species = matrices.shape[0]
    numbers = jnp.arange(species, dtype=jnp.int32)

    def eliminate(pivot_index, current):
        pivot_row = lax.dynamic_index_in_dim(current, pivot_index, 0, keepdims=False)
        pivot_column = lax.dynamic_index_in_dim(current, pivot_index, 1, keepdims=False)
        pivot_value = lax.dynamic_index_in_dim(pivot_row, pivot_index, 0, keepdims=False)
        is_pivot = numbers == pivot_index
        scaled = jnp.where(is_pivot[:, None], 1.0, pivot_row) / pivot_value[None, :]
        weights = jnp.where(is_pivot[:, None], 0.0, pivot_column)
        cleared = jnp.where(is_pivot[None, :, None], 0.0, current)
        updated = cleared - weights[:, None, :] * scaled[None, :, :]
        return jnp.where(is_pivot[:, None, None], scaled[None, :, :], updated)

    return lax.fori_loop(0, species, eliminate, matrices)


def invert_blocked(matrices):
    species = matrices.shape[0]
    cell_count = matrices.shape[2]
    block_width = 128
    blocks = matrices.reshape(species, species, cell_count // block_width, block_width).transpose(
        2, 0, 1, 3
    )
    inverted = lax.map(invert, blocks)
    return inverted.transpose(1, 2, 0, 3).reshape(species, species, cell_count)


def apply_inverse(inverse_table, vector):
    return jnp.einsum("ijc,jc->ic", inverse_table.astype(jnp.float32), vector, precision=precise)


def rows_around(field_now, columns):
    return extended(field_now, (("space", 1),), columns)


def to_next(field_now):
    return passed_along(field_now, "tm", 1)


def per_device(initial_field, decay_rates, source, diffusion, saturation, conversion):
    columns = COLS
    cell_count = initial_field.shape[1]
    off_diagonal, outflow = conversion_parts(conversion)
    fine_table = invert_blocked(
        jacobian(1.0, decay_rates, diffusion, off_diagonal, outflow)
    ).astype(jnp.bfloat16)
    coarse_table = invert_blocked(
        jacobian(float(FACTOR), decay_rates, diffusion, off_diagonal, outflow)
    ).astype(jnp.bfloat16)
    is_anchor = lax.axis_index("tm") == 0
    space_index = lax.axis_index("space")
    space_count = lax.axis_size("space")
    link_count = lax.axis_size("tm") - 1

    def local_force(padded):
        return tendency(
            padded, columns, decay_rates, source, diffusion, saturation, off_diagonal, outflow
        )

    def fine_step(previous):
        iterate = previous
        for newton_turn in range(NEWTON):
            defect = iterate - previous - local_force(rows_around(iterate, columns))
            iterate = iterate - apply_inverse(fine_table, defect)
        return iterate

    def propagate(field_now):
        for fine_turn in range(FACTOR):
            field_now = fine_step(field_now)
        return field_now

    points = initial_field
    for cycle_index in range(CYCLES):
        reached = to_next(propagate(points))
        points = jnp.where(is_anchor, initial_field, reached)
        interval_end = propagate(points)
        coarse_here = points + FACTOR * apply_inverse(
            coarse_table, local_force(rows_around(points, columns))
        )
        incoming = to_next(interval_end - coarse_here)

        def strip_link(round_index, carried):
            strip_value = passed_along(carried, ("tm", "space"), space_count)
            upper_rim = passed_along(
                carried[:, cell_count - columns :], ("tm", "space"), space_count + 1
            )
            lower_rim = passed_along(strip_value[:, :columns], "space", -1)
            upper_rim = jnp.where(space_index == 0, 0.0, upper_rim)
            padded = jnp.concatenate([upper_rim, strip_value, lower_rim], axis=1)
            advanced = (
                strip_value + FACTOR * apply_inverse(coarse_table, local_force(padded)) + incoming
            )
            return jnp.where(is_anchor, initial_field, advanced)

        points = lax.fori_loop(0, link_count, strip_link, points)
    return points[None]


def solution(mesh):
    in_specs = (P(None, "space"), P(None, "space"), P(None, "space"), P(), P(), P())
    out_specs = P("tm", None, "space")
    return jax.shard_map(
        per_device, mesh=mesh, in_specs=in_specs, out_specs=out_specs, check_vma=False
    )
```

profile of v0, /device:TPU:97, one launch (start us, length us, event | category | flops | bytes accessed | tf_op | source)
XLA Modules:
  0.0 1805.0 jit_solution(15978480143778064580)
XLA Ops:
  14.2 140.0 %while.101 = (s32[]{:T(128)}, bf16[4,48,48,128]{3,2,1,0:T(8,128)(2,1)S(1)}, f32[4,48,48,128]{3,2,1,0:T(8,128)}, s32[]{:T(128)}, s32[]{:T(128)}, /*index=5*/s32[]{:T(128)}, s32[]{:T(128)}, s32[]{:T(128)}) while((s32[]{:T(128)}, bf16[4,48,48,128]{3,2,1,0:T(8,128)(2,1)S(1)}, f32[4,48,48,128]{3,2,1,0:T(8,128)}, s32[]{:T(128)}, s32[]{:T(128)}, ...), condition=%wide.region_4.5_spmd, body=%wide.region_1.4_spmd.sunk | while | flops 1198133 | bytes 7227306 | solution.py:101
  15.6 33.5 %while.106 = (s32[]{:T(128)}, f32[48,48,128]{2,1,0:T(8,128)S(1)}, s32[]{:T(128)}, s32[]{:T(128)}, s32[]{:T(128)}) while((s32[]{:T(128)}, f32[48,48,128]{2,1,0:T(8,128)S(1)}, s32[]{:T(128)}, s32[]{:T(128)}, s32[]{:T(128)}) %tuple.231), condition=%wide.region_3.3_spmd.clone, body=%wide.region_2.2_spmd.clone.sunk | while | flops 1198131 | bytes 2508573 | solution.py:91
  50.6 33.5 %while.106 = (s32[]{:T(128)}, f32[48,48,128]{2,1,0:T(8,128)S(1)}, s32[]{:T(128)}, s32[]{:T(128)}, s32[]{:T(128)}) while((s32[]{:T(128)}, f32[48,48,128]{2,1,0:T(8,128)S(1)}, s32[]{:T(128)}, s32[]{:T(128)}, s32[]{:T(128)}) %tuple.231), condition=%wide.region_3.3_spmd.clone, body=%wide.region_2.2_spmd.clone.sunk | while | flops 1198131 | bytes 2508573 | solution.py:91
  85.6 33.5 %while.106 = (s32[]{:T(128)}, f32[48,48,128]{2,1,0:T(8,128)S(1)}, s32[]{:T(128)}, s32[]{:T(128)}, s32[]{:T(128)}) while((s32[]{:T(128)}, f32[48,48,128]{2,1,0:T(8,128)S(1)}, s32[]{:T(128)}, s32[]{:T(128)}, s32[]{:T(128)}) %tuple.231), condition=%wide.region_3.3_spmd.clone, body=%wide.region_2.2_spmd.clone.sunk | while | flops 1198131 | bytes 2508573 | solution.py:91
  120.6 33.5 %while.106 = (s32[]{:T(128)}, f32[48,48,128]{2,1,0:T(8,128)S(1)}, s32[]{:T(128)}, s32[]{:T(128)}, s32[]{:T(128)}) while((s32[]{:T(128)}, f32[48,48,128]{2,1,0:T(8,128)S(1)}, s32[]{:T(128)}, s32[]{:T(128)}, s32[]{:T(128)}) %tuple.231), condition=%wide.region_3.3_spmd.clone, body=%wide.region_2.2_spmd.clone.sunk | while | flops 1198131 | bytes 2508573 | solution.py:91
  284.2 143.0 %while.103 = (s32[]{:T(128)}, bf16[4,48,48,128]{3,2,1,0:T(8,128)(2,1)}, f32[4,48,48,128]{3,2,1,0:T(8,128)}, s32[]{:T(128)}, s32[]{:T(128)}, /*index=5*/s32[]{:T(128)}, s32[]{:T(128)}, s32[]{:T(128)}) while((s32[]{:T(128)}, bf16[4,48,48,128]{3,2,1,0:T(8,128)(2,1)}, f32[4,48,48,128]{3,2,1,0:T(8,128)}, s32[]{:T(128)}, s32[]{:T(128)}, ...), condition=%wide.region_8.9_spmd, body=%wide.region_5.8_spmd.sunk | while | flops 1198133 | bytes 7227814 | solution.py:101
  285.5 33.5 %while.107 = (s32[]{:T(128)}, f32[48,48,128]{2,1,0:T(8,128)S(1)}, s32[]{:T(128)}, s32[]{:T(128)}, s32[]{:T(128)}) while((s32[]{:T(128)}, f32[48,48,128]{2,1,0:T(8,128)S(1)}, s32[]{:T(128)}, s32[]{:T(128)}, s32[]{:T(128)}) %tuple.228), condition=%wide.region_7.7_spmd.clone, body=%wide.region_6.6_spmd.clone.sunk | while | flops 1198131 | bytes 2508573 | solution.py:91
  321.3 33.5 %while.107 = (s32[]{:T(128)}, f32[48,48,128]{2,1,0:T(8,128)S(1)}, s32[]{:T(128)}, s32[]{:T(128)}, s32[]{:T(128)}) while((s32[]{:T(128)}, f32[48,48,128]{2,1,0:T(8,128)S(1)}, s32[]{:T(128)}, s32[]{:T(128)}, s32[]{:T(128)}) %tuple.228), condition=%wide.region_7.7_spmd.clone, body=%wide.region_6.6_spmd.clone.sunk | while | flops 1198131 | bytes 2508573 | solution.py:91
  357.0 33.5 %while.107 = (s32[]{:T(128)}, f32[48,48,128]{2,1,0:T(8,128)S(1)}, s32[]{:T(128)}, s32[]{:T(128)}, s32[]{:T(128)}) while((s32[]{:T(128)}, f32[48,48,128]{2,1,0:T(8,128)S(1)}, s32[]{:T(128)}, s32[]{:T(128)}, s32[]{:T(128)}) %tuple.228), condition=%wide.region_7.7_spmd.clone, body=%wide.region_6.6_spmd.clone.sunk | while | flops 1198131 | bytes 2508573 | solution.py:91
  392.8 33.5 %while.107 = (s32[]{:T(128)}, f32[48,48,128]{2,1,0:T(8,128)S(1)}, s32[]{:T(128)}, s32[]{:T(128)}, s32[]{:T(128)}) while((s32[]{:T(128)}, f32[48,48,128]{2,1,0:T(8,128)S(1)}, s32[]{:T(128)}, s32[]{:T(128)}, s32[]{:T(128)}) %tuple.228), condition=%wide.region_7.7_spmd.clone, body=%wide.region_6.6_spmd.clone.sunk | while | flops 1198131 | bytes 2508573 | solution.py:91
  448.3 604.1 %while.104 = (s32[]{:T(128)}, f32[48,512]{1,0:T(8,128)S(1)}, pred[]{:T(512)}, f32[48]{0:T(128)S(1)}, pred[]{:T(512)}, /*index=5*/f32[48,48]{1,0:T(8,128)S(1)}, f...) while((s32[]{:T(128)}, f32[48,512]{1,0:T(8,128)S(1)}, ...), condition=%wide.region_10.11_spmd, body=%wide.region_9.10_spmd.sunk | while | flops 18294784 | bytes 4771583 | solution.py:172
  452.2 7.7 collective-permute-done.1
  471.6 7.7 collective-permute-done.1
  491.0 7.7 collective-permute-done.1
  510.5 7.7 collective-permute-done.1
  549.3 7.7 collective-permute-done.1
  608.2 7.7 collective-permute-done.1
  628.6 7.7 collective-permute-done.1
  667.8 7.7 collective-permute-done.1
  706.6 7.7 collective-permute-done.1
  745.5 7.7 collective-permute-done.1
  1118.3 8.0 collective-permute-done.56
  1194.0 7.9 collective-permute-done.73
  1202.0 602.0 %while.105 = (s32[]{:T(128)}, f32[48,512]{1,0:T(8,128)S(1)}, pred[]{:T(512)}, f32[48]{0:T(128)S(1)}, pred[]{:T(512)}, /*index=5*/f32[48,48]{1,0:T(8,128)S(1)}, f...) while((s32[]{:T(128)}, f32[48,512]{1,0:T(8,128)S(1)}, ...), condition=%wide.region_12.13_spmd, body=%wide.region_11.12_spmd.sunk | while | flops 18294784 | bytes 4771583 | solution.py:172
  (3189 shorter events, 1685.9 us)
Async XLA Ops:
  1.4 152.9 %collective-permute-start.6 = (f32[48,128]{1,0:T(8,128)}, f32[48,128]{1,0:T(8,128)}, u32[]{:S(2)}, u32[]{:S(2)}) collective-permute-start(f32[48,128]{1,0:T(8,128)} %get-tuple-element.803), channel_id=1, source_target_pairs={{0,1},{1,2},{2,3},{4,5},{5,6},{6,7},{8,9},{9,10},{10,11},{12,13},{... | collective-permute-start | bytes 73736 | tf_op jit(solution)/shard_map/ppermute | solution.py:22
  5.1 150.9 %collective-permute-start.7 = (f32[48,128]{1,0:T(8,128)}, f32[48,128]{1,0:T(8,128)}, u32[]{:S(2)}, u32[]{:S(2)}) collective-permute-start(f32[48,128]{1,0:T(8,128)} %get-tuple-element.804), channel_id=1, source_target_pairs={{1,0},{2,1},{3,2},{5,4},{6,5},{7,6},{9,8},{10,9},{11,10},{13,12},{... | collective-permute-start | bytes 73736 | tf_op jit(solution)/shard_map/ppermute | solution.py:23
  277.5 149.7 %collective-permute-start.35 = (f32[48,128]{1,0:T(8,128)}, f32[48,128]{1,0:T(8,128)}, u32[]{:S(2)}, u32[]{:S(2)}) collective-permute-start(f32[48,128]{1,0:T(8,128)} %get-tuple-element.773), channel_id=1, source_target_pairs={{0,1},{1,2},{2,3},{4,5},{5,6},{6,7},{8,9},{9,10},{10,11},{12,13},{... | collective-permute-start | bytes 73736 | tf_op jit(solution)/shard_map/ppermute | solution.py:22
  279.4 147.8 %collective-permute-start.36 = (f32[48,128]{1,0:T(8,128)}, f32[48,128]{1,0:T(8,128)}, u32[]{:S(2)}, u32[]{:S(2)}) collective-permute-start(f32[48,128]{1,0:T(8,128)} %get-tuple-element.774), channel_id=1, source_target_pairs={{1,0},{2,1},{3,2},{5,4},{6,5},{7,6},{9,8},{10,9},{11,10},{13,12},{... | collective-permute-start | bytes 73736 | tf_op jit(solution)/shard_map/ppermute | solution.py:23
  467.7 11.6 collective-permute-start
  487.2 11.6 collective-permute-start
  506.6 11.6 collective-permute-start
  526.0 11.6 collective-permute-start
  545.4 11.6 collective-permute-start
  564.9 11.6 collective-permute-start
  584.3 11.6 collective-permute-start
  604.3 11.6 collective-permute-start
  624.8 11.6 collective-permute-start
  644.4 11.6 collective-permute-start
  663.9 11.6 collective-permute-start
  683.3 11.6 collective-permute-start
  702.7 11.6 collective-permute-start
  722.2 11.6 collective-permute-start
  741.6 11.6 collective-permute-start
  761.0 11.6 collective-permute-start
  780.4 11.6 collective-permute-start
  799.9 11.6 collective-permute-start
  877.6 11.6 collective-permute-start
  1745.7 11.6 collective-permute-start.3
  (253 other events, 2299.1 us)
where the time goes:
time: 1820 us; the launch traced here: 1810 us
  waiting for transfers between devices  790 us (43%)
  starting transfers between devices  510 us (28%)
  other arithmetic  423 us (23%)
  local copies, waits for them, and re-layouts  31 us (2%)
  matrix products  25.3 us (1%)
  loops' own time  23.5 us (1%)
    ppermute x190, waiting for transfers between devices, passed_along(): return lax.ppermute(block, axis, route)  708 us
    ppermute x190, starting transfers between devices, passed_along(): return lax.ppermute(block, axis, route)  366 us
    select_n x384, other arithmetic, eliminate(): return jnp.where(is_pivot[:, None, None], scaled[None, :, :], updated)  168 us
    dot_general x96, other arithmetic, apply_inverse(): jnp.einsum('ijc,jc->ic', inverse_table.astype(jnp.float32), vector, preci...  167 us
    ppermute x32, waiting for transfers between devices, extended(): after = lax.ppermute(initial, axis, down)  82.2 us
    ppermute x32, starting transfers between devices, extended(): after = lax.ppermute(initial, axis, down)  75.6 us
    ppermute x32, starting transfers between devices, extended(): before = lax.ppermute(last, axis, up)  68.1 us
    select_n x384, other arithmetic, eliminate(): weights = jnp.where(is_pivot[:, None], 0.0, pivot_column)  44.5 us
  transfers between devices with their start and end apart: 254, of which 158 were waited for; matrix products, arithmetic and copies ran while one was open for 16% of the time, Pallas kernels for 0%

commit v1 on v0

v1 whole, which is shorter than its diff:
```python
import functools

import jax
import jax.numpy as jnp
from jax import lax
from jax.experimental import pallas as pl
from jax.experimental.pallas import tpu as pltpu
from jax.sharding import PartitionSpec as P

COLS = 128
FACTOR = 4
NEWTON = 2
ROWS = 16
CELLS = 2048
S = 48
TILE = 256
CENTRE = 0.4
ENOUGH = 2e-4
GROUP = 4

VMEM = pl.BlockSpec(memory_space=pltpu.VMEM)
ANY = pl.BlockSpec(memory_space=pl.ANY)
TILES = [slice(start, start + TILE) for start in range(0, CELLS, TILE)]
SMEM = pl.BlockSpec(memory_space=pltpu.SMEM)
PARAMS = pltpu.CompilerParams(vmem_limit_bytes=48 << 20)


def halves(value):
    high = value.astype(jnp.bfloat16)
    low = (value - high.astype(jnp.float32)).astype(jnp.bfloat16)
    return high, low


def stacked(value):
    high, low = halves(value)
    return jnp.concatenate([high, low, high], axis=0)


def wide(matrix):
    rounded = lax.reduce_precision(matrix, 8, 7)
    high, low = rounded.astype(jnp.bfloat16), (matrix - rounded).astype(jnp.bfloat16)
    return jnp.concatenate([high, high, low], axis=1)


def times(matrix, value):
    return jnp.dot(matrix, stacked(value), preferred_element_type=jnp.float32)


def invert_kernel(matrix_ref, out_ref, first_mode, second_mode):
    lane = lax.broadcasted_iota(jnp.int32, (S, COLS), 1)
    row_number = lax.broadcasted_iota(jnp.int32, (S, COLS), 0)
    lane_row = lax.broadcasted_iota(jnp.int32, (1, COLS), 1)
    out_ref[...] = matrix_ref[...]

    def eliminate(k, _):
        current = out_ref[...]
        row = out_ref[pl.ds(k, 1), :]
        first = jnp.sum(jnp.where(lane == k, current, 0.0), axis=1, keepdims=True)
        second = jnp.sum(jnp.where(lane == k + 64, current, 0.0), axis=1, keepdims=True)
        pivot_first = jnp.sum(jnp.where(lane_row == k, row, 0.0), axis=1, keepdims=True)
        pivot_second = jnp.sum(jnp.where(lane_row == k + 64, row, 0.0), axis=1, keepdims=True)
        column = jnp.where(lane < 64, first, second)
        pivot = jnp.where(lane_row < 64, pivot_first, pivot_second)
        at_row = (lane_row == k) | (lane_row == k + 64)
        scaled = jnp.where(at_row, 1.0, row) / pivot
        weights = jnp.where(row_number == k, 0.0, column)
        cleared = jnp.where((lane == k) | (lane == k + 64), 0.0, current)
        updated = cleared - weights * scaled
        out_ref[...] = jnp.where(row_number == k, scaled, updated)
        return 0

    lax.fori_loop(0, S, eliminate, 0)
    for at, mode in ((0, first_mode), (64, second_mode)):
        power = out_ref[:, at : at + S]
        for _ in range(2):
            power = jnp.dot(power, power, precision=lax.Precision.HIGHEST, preferred_element_type=jnp.float32)
        mode[...] = jnp.sum(power, axis=1, keepdims=True)


def invert_pair(first, second):
    gap = jnp.zeros((S, 16), jnp.float32)
    pair = jnp.concatenate([first, gap, second, gap], axis=1)
    pair = pair + jnp.where(jnp.arange(COLS) % 64 >= S, 1.0, 0.0)[None, :]
    column = jax.ShapeDtypeStruct((S, 1), jnp.float32)
    inverted, first_mode, second_mode = pl.pallas_call(
        invert_kernel,
        out_shape=[jax.ShapeDtypeStruct((S, COLS), jnp.float32), column, column],
        in_specs=[VMEM],
        out_specs=[VMEM] * 3,
        name="invert_pair",
    )(pair)
    return inverted[:, :S], inverted[:, 64 : 64 + S], first_mode, second_mode


class Solver:
    def __init__(self, inverse, mode, balance):
        self.inverse, self.balance = inverse, balance
        self.mode = jnp.broadcast_to(mode[...], (S, TILE))


class Grid:
    def __init__(self, rate, delta, source, spread, saturation, mixing, residual, change):
        self.rate, self.delta, self.source = rate, delta, source
        self.spread = jnp.broadcast_to(spread[...], (S, COLS))
        self.saturation = jnp.broadcast_to(saturation[...], (S, COLS))
        self.mixing, self.residual, self.change = mixing, residual, change
        lane = lax.broadcasted_iota(jnp.int32, (S, COLS), 1)
        self.not_first, self.not_last = lane != 0, lane != COLS - 1

    def force_row(self, field, r, mixed):
        at = slice(r * COLS, (r + 1) * COLS)
        here = field[:, at]
        around = jnp.where(self.not_first, pltpu.roll(here, 1, 1), 0.0) + jnp.where(
            self.not_last, pltpu.roll(here, COLS - 1, 1), 0.0
        )
        if r > 0:
            around = around + field[:, (r - 1) * COLS : r * COLS]
        if r < ROWS - 1:
            around = around + field[:, (r + 1) * COLS : (r + 2) * COLS]
        saturated = self.saturation * here / (1.0 + here * here)
        return self.spread * around + mixed - self.rate[:, at] * here + saturated + self.source[:, at]

    def force(self, field, at):
        mixed = times(self.mixing[...], field[:, at])
        r = at.start // COLS
        return jnp.concatenate(
            [self.force_row(field, r + k, mixed[:, k * COLS : (k + 1) * COLS]) for k in range(2)],
            axis=1,
        )

    def turn(self, solver, at, value, before):
        change = times(solver.inverse[...], value)
        left = self.delta[:, at] * (change if before is None else change - before)
        share = jnp.sum(left, axis=0, keepdims=True) * solver.balance[:, at]
        return change + solver.mode * share, left

    def solve(self, solver, field, previous, count, finish):
        for at in TILES:
            value = self.force(field, at)
            if previous is not None:
                value = value + (previous[:, at] - field[:, at])
            self.residual[:, at] = value
            self.change[:, at] = self.turn(solver, at, value, None)[0]

        def next_turn(at):
            before = self.change[:, at]
            return self.turn(solver, at, self.residual[:, at] + self.delta[:, at] * before, before)

        def middle(_, carry):
            for at in TILES:
                self.change[:, at] = next_turn(at)[0]
            return carry

        lax.fori_loop(2, count, middle, 0)
        for at in TILES:
            finish(at, *next_turn(at))

    def fine_steps(self, solver, field, previous, count):
        def first(at, change, _):
            here = field[:, at]
            previous[:, at] = here
            field[:, at] = here + change

        def second(at, change, _):
            field[:, at] = field[:, at] + change

        def step(_, carry):
            self.solve(solver, field, None, count, first)
            self.solve(solver, field, previous, count, second)
            return carry

        lax.fori_loop(0, FACTOR, step, 0)


def main_kernel(
    where, own, beside, across, corner, fine, coarse, fine_mode, coarse_mode,
    mixing, spread, saturation, still,
    half, rest, first, rate, delta, source, balance, counts,
    field, previous, keep, residual, change, fine_balance,
):
    interval, strip = where[0], where[1]
    width = own.shape[1]
    pieces = (own, beside, across, corner)

    def place(k):
        return pl.ds(pl.multiple_of(jnp.bitwise_xor(strip, k) * width, COLS), width)

    for k, piece in enumerate(pieces):
        decay = piece[S : 2 * S, :]
        delta[:, place(k)] = CENTRE - decay
        rate[:, place(k)] = still[...] + decay
        source[:, place(k)] = piece[2 * S : 3 * S, :]
        for mode, shift, total in ((fine_mode, 1.0, fine_balance), (coarse_mode, 1.0 / FACTOR, balance)):
            losses = (shift + 4.0 * spread[...] + decay) * mode[...]
            total[:, place(k)] = 1.0 / jnp.sum(losses, axis=0, keepdims=True)
    grid = Grid(rate, delta, source, spread, saturation, mixing, residual, change)
    fine_solver = Solver(fine, fine_mode, fine_balance)
    coarse_solver = Solver(coarse, coarse_mode, balance)

    def own_strip():
        return field[:, pl.ds(pl.multiple_of(strip * width, COLS), width)]

    def attempt(state):
        fine_count, coarse_count = 2 << state[0], 3 << state[0]
        counts[0], counts[1] = fine_count, coarse_count
        for k, piece in enumerate(pieces):
            field[:, place(k)] = piece[0:S, :]
        first[0] = own_strip()
        grid.fine_steps(fine_solver, field, previous, fine_count)
        first[1] = own_strip()
        for at in TILES:
            keep[:, at] = field[:, at]
        grid.fine_steps(fine_solver, field, previous, fine_count)
        first[2] = own_strip()
        errors, squares = [], []

        def defect(at, moved, left):
            here = field[:, at]
            rest_of = here - keep[:, at] - moved
            previous[:, at] = rest_of
            errors.append(left * left)
            squares.append(here * here)

        grid.solve(coarse_solver, keep, None, coarse_count, defect)
        error, square = jnp.sum(sum(errors)), jnp.sum(sum(squares))
        return state[0] + 1, error <= (ENOUGH * ENOUGH) * square

    lax.while_loop(lambda state: jnp.logical_not(state[1]) & (state[0] < 6), attempt, (jnp.int32(0), False))
    fine_count, coarse_count = counts[0], counts[1]

    @pl.when(interval <= 3)
    def _():
        for at in TILES:
            field[:, at] = keep[:, at]

    for at in TILES:
        keep[:, at] = previous[:, at]

    def linked(at, moved, _):
        field[:, at] = field[:, at] + moved + keep[:, at]

    def link(_, carry):
        grid.solve(coarse_solver, field, None, coarse_count, linked)
        return carry

    lax.fori_loop(4, interval, link, 0)
    grid.fine_steps(fine_solver, field, previous, fine_count)
    for at in TILES:
        keep[:, at] = field[:, at]
    grid.fine_steps(fine_solver, field, previous, fine_count)

    def handed(at, moved, _):
        previous[:, at] = field[:, at] - jnp.where(interval <= 3, 0.0, keep[:, at] + moved)

    grid.solve(coarse_solver, keep, None, coarse_count, handed)
    half[...] = previous[:, half_at(strip, 0)]
    rest[...] = previous[:, half_at(strip, 1)]


def half_at(strip, other):
    core = jnp.bitwise_xor(jnp.bitwise_and(strip, 1), other)
    return pl.ds(pl.multiple_of(core * (CELLS // 2), COLS), CELLS // 2)


def whole():
    return jax.ShapeDtypeStruct((S, CELLS), jnp.float32)


def half_grid():
    return jax.ShapeDtypeStruct((S, CELLS // 2), jnp.float32)


def line():
    return jax.ShapeDtypeStruct((1, CELLS), jnp.float32)


def scratch(count):
    return [pltpu.VMEM((S, CELLS), jnp.float32) for _ in range(count)]


def run_main(where, pieces, *shared):
    width = pieces[0].shape[1]
    return pl.pallas_call(
        main_kernel,
        out_shape=[
            half_grid(), half_grid(), jax.ShapeDtypeStruct((3, S, width), jnp.float32),
            whole(), whole(), whole(), line(), jax.ShapeDtypeStruct((2,), jnp.int32),
        ],
        in_specs=[SMEM] + [VMEM] * 12,
        out_specs=[VMEM] * 7 + [SMEM],
        scratch_shapes=scratch(5) + [pltpu.VMEM((1, CELLS), jnp.float32)],
        compiler_params=PARAMS,
        name="to_payload",
    )(where, *pieces, *shared)


def chain_kernel(*refs):
    where, counts = refs[:2]
    arrived, payloads = refs[2:4], refs[4 : 4 + 2 * GROUP]
    rest = refs[4 + 2 * GROUP :]
    coefficients = rest[:3]
    coarse, mode, balance, mixing, spread, saturation = rest[3:9]
    half, mine, field, residual, change, rate, delta, source, stage, fetched, passed = rest[9:]
    member, strip = where[0] % GROUP, where[1]
    width = mine.shape[1]
    copies = [pltpu.make_async_copy(arrived[k], field.at[:, half_at(strip, k)], fetched.at[k]) for k in range(2)]
    copies += [
        pltpu.make_async_copy(source_ref, target, fetched.at[2 + k])
        for k, (source_ref, target) in enumerate(zip(coefficients, (rate, delta, source)))
    ]
    held = []
    for j in range(GROUP):
        slot = (member + j) % GROUP
        held.append([
            pltpu.make_async_copy(
                payloads[2 * j + k], stage.at[slot, :, half_at(strip, k)], passed.at[slot, k]
            )
            for k in range(2)
        ])
    for copy in copies + sum(held, []):
        copy.start()
    for copy in copies:
        copy.wait()
    grid = Grid(rate, delta, source, spread, saturation, mixing, residual, change)
    solver = Solver(coarse, mode, balance)
    for pair in held:
        for copy in pair:
            copy.wait()

    def link(k, carry):
        def linked(at, moved, _):
            field[:, at] = field[:, at] + moved + stage[k, :, at]

        grid.solve(solver, field, None, counts[1], linked)

        @pl.when(member == k)
        def _():
            mine[...] = field[:, pl.ds(pl.multiple_of(strip * width, COLS), width)]

        return carry

    lax.fori_loop(0, GROUP, link, 0)
    half[...] = field[:, half_at(strip, 0)]


def run_chain(where, counts, arrived, payloads, coefficients, shared):
    return pl.pallas_call(
        chain_kernel,
        out_shape=[half_grid(), jax.ShapeDtypeStruct((S, CELLS // 4), jnp.float32)],
        in_specs=[SMEM, SMEM] + [ANY] * (2 + 2 * GROUP + 3) + [VMEM] * 6,
        out_specs=[VMEM, VMEM],
        scratch_shapes=scratch(6)
        + [
            pltpu.VMEM((GROUP, S, CELLS), jnp.float32),
            pltpu.SemaphoreType.DMA((5,)),
            pltpu.SemaphoreType.DMA((GROUP, 2)),
        ],
        compiler_params=PARAMS,
        name="links",
    )(where, counts, *arrived, *payloads, *coefficients, *shared)


def neighbour_route():
    route = []
    for tm in range(32):
        for strip in range(4):
            high, low, core = (tm // 4) % 2, strip // 2, strip % 2
            y = high * 2 + low
            from_y = (y + 1) % 4 if core else (y - 1) % 4
            from_tm = tm + ((from_y // 2) - high) * 4
            route.append((from_tm * 4 + (from_y % 2) * 2 + core, tm * 4 + strip))
    return route


def per_device(initial_field, decay_rates, source, diffusion, saturation, conversion):
    strip, interval = lax.axis_index("space"), lax.axis_index("tm")
    where = jnp.stack([interval, strip]).astype(jnp.int32)
    own = jnp.concatenate([initial_field, decay_rates, source], axis=0)
    swap = [(0, 1), (1, 0), (2, 3), (3, 2)]
    across = lax.ppermute(own, ("tm", "space"), neighbour_route())
    beside = lax.ppermute(own, "space", swap)
    corner = lax.ppermute(across, "space", swap)

    off_diagonal = conversion * (1.0 - jnp.eye(S, dtype=jnp.float32))
    outflow = jnp.sum(off_diagonal, axis=0)
    still = 4.0 * diffusion + outflow
    centre = jnp.eye(S, dtype=jnp.float32) * (still + CENTRE)[:, None] - off_diagonal
    fine, coarse, fine_mode, coarse_mode = invert_pair(
        centre + jnp.eye(S, dtype=jnp.float32), centre + jnp.eye(S, dtype=jnp.float32) / FACTOR
    )
    fine, coarse, mixing = wide(fine), wide(coarse), wide(off_diagonal)
    spread, saturation, still = diffusion[:, None], saturation[:, None], (still + saturation)[:, None]
    half, rest, first, *coefficients, balance, counts = run_main(
        where, (own, beside, across, corner), fine, coarse, fine_mode, coarse_mode,
        mixing, spread, saturation, still,
    )
    shared = (coarse, coarse_mode, balance, mixing, spread, saturation)
    in_group = [half, rest]
    for distance in range(1, GROUP):
        route = [(i // GROUP * GROUP + (i + distance) % GROUP, i) for i in range(32)]
        arrived = lax.ppermute(half, "tm", route)
        in_group += [arrived, lax.ppermute(arrived, "space", swap)]
    group, member = interval // GROUP, interval % GROUP
    last = half
    for j in range(1, GROUP):
        last = jnp.where((member + j) % GROUP == GROUP - 1, in_group[2 * j], last)
    width = initial_field.shape[1]
    both = jnp.where(strip % 2 == strip // 2, half, rest)
    third = lax.dynamic_slice_in_dim(both, (strip % 2) * width, width, axis=1)
    mine = jnp.where(
        interval == 0, first[0], jnp.where(interval == 1, first[1], jnp.where(interval == 2, first[2], third))
    )
    for hop in range(32 // GROUP - 1):
        route = [(hop * GROUP + m, (hop + 1) * GROUP + m) for m in range(GROUP)]
        arrived = lax.ppermute(last, "tm", route)
        arrived = (arrived, lax.ppermute(arrived, "space", swap))

        def active(arrived=arrived):
            return tuple(run_chain(where, counts, arrived, in_group, coefficients, shared))

        last, mine = lax.cond(group == hop + 1, active, lambda: (last, mine))
    return mine[None]


def solution(mesh):
    in_specs = (P(None, "space"), P(None, "space"), P(None, "space"), P(), P(), P())
    out_specs = P("tm", None, "space")
    return jax.shard_map(
        per_device, mesh=mesh, in_specs=in_specs, out_specs=out_specs, check_vma=False
    )
```

time: 1820 us -> 181 us (0.10)
  the two profiles are of different devices: /device:TPU:97 before, /device:TPU:113 now
where the time goes in v1:
time: 181 us
  waiting for transfers between devices  84.7 us (47%)
  Pallas kernels  71.3 us (39%)
  starting transfers between devices  18.9 us (10%)
  local copies, waits for them, and re-layouts  3.47 us (2%)
  other arithmetic  1.88 us (1%)
    ppermute x7, waiting for transfers between devices, per_device(): arrived = lax.ppermute(last, 'tm', route)  67.1 us
    pallas_call x1, Pallas kernels, run_main(): pl.pallas_call(main_kernel, out_shape=[half_grid(), half_grid(), jax.Shap...  57.9 us
    ppermute x3, waiting for transfers between devices, per_device(): arrived = lax.ppermute(half, 'tm', route)  9.1 us
    ppermute x3, starting transfers between devices, per_device(): arrived = lax.ppermute(half, 'tm', route)  7.18 us
    ppermute x7, waiting for transfers between devices, per_device(): arrived = (arrived, lax.ppermute(arrived, 'space', swap))  7.15 us
    pallas_call x1, Pallas kernels, run_chain(): pl.pallas_call(chain_kernel, out_shape=[half_grid(), jax.ShapeDtypeStruct...  6.9 us
    pallas_call x1, Pallas kernels, invert_pair(): pl.pallas_call(invert_kernel, out_shape=[jax.ShapeDtypeStruct((S, COLS),...  6.5 us
    ppermute x7, starting transfers between devices, per_device(): arrived = lax.ppermute(last, 'tm', route)  5.26 us
  transfers between devices with their start and end apart: 23, of which 13 were waited for; matrix products, arithmetic and copies ran while one was open for 1% of the time, Pallas kernels for 4%

profile of v1, /device:TPU:113, one launch (start us, length us, event | category | flops | bytes accessed | tf_op | source)
XLA Modules:
  0.0 180.7 jit_solution(1326912074274074445)
XLA Ops:
  0.0 0.9 constant_dynamic-update-slice_fusion.2
  1.0 0.9 copy-done.3
  2.1 1.8 collective-permute-start
  4.6 0.7 maximum_add_fusion.matrix_ref
  5.3 6.5 %invert_pair.1 = (f32[48,128]{1,0:T(8,128)}, f32[48,1]{1,0:T(8,128)}, f32[48,1]{1,0:T(8,128)S(1)}) custom-call(f32[48,128]{1,0:T(8,128)} %maximum_add_fusion.matrix_ref), custom_call_target="tpu_custom_call" | custom-call | tf_op jit(solution)/shard_map/invert_pair/pallas_call | solution.py:85
  13.1 0.8 collective-permute-done.2.corner
  14.0 57.9 %to_payload.1 = (f32[48,1024]{1,0:T(8,128)S(1)}, f32[48,1024]{1,0:T(8,128)S(1)}, f32[3,48,512]{2,1,0:T(8,128)S(1)}, f32[48,2048]{1,0:T(8,128)S(1)}, f32[48,2048]...) custom-call(s32[2]{0:T(128)S(1)} %pad_add_fusion.where, ...), custom_call_target="tpu_custom_call" | custom-call | tf_op jit(solution)/shard_map/to_payload/pallas_call | solution.py:283
  71.9 2.4 %collective-permute-start.3 = (f32[48,1024]{1,0:T(8,128)S(1)}, f32[48,1024]{1,0:T(8,128)S(1)}, u32[]{:S(2)}, u32[]{:S(2)}) collective-permute-start(f32[48,1024]{1,0:T(8,128)S(1)} %get-tuple-element.503), channel_id=1, source_target_pairs={{12,0},{0,4},{4,8},{8,12},{28,16},{16,20},{20,24},{24,28},{44,32},... | collective-permute-start | bytes 589832 | tf_op jit(solution)/shard_map/ppermute | solution.py:401
  74.3 4.7 %collective-permute-start.4 = (f32[48,1024]{1,0:T(8,128)S(1)}, f32[48,1024]{1,0:T(8,128)S(1)}, u32[]{:S(2)}, u32[]{:S(2)}) collective-permute-start(f32[48,1024]{1,0:T(8,128)S(1)} %get-tuple-element.503), channel_id=1, source_target_pairs={{8,0},{12,4},{0,8},{4,12},{24,16},{28,20},{16,24},{20,28},{40,32},... | collective-permute-start | bytes 589832 | tf_op jit(solution)/shard_map/ppermute | solution.py:401
  79.1 3.9 %collective-permute-done.3 = f32[48,1024]{1,0:T(8,128)S(1)} collective-permute-done((f32[48,1024]{1,0:T(8,128)S(1)}, f32[48,1024]{1,0:T(8,128)S(1)}, u32[]{:S(2)}, u32[]{:S(2)}) %collective-permute-start.3) | collective-permute-done | bytes 196640 | tf_op jit(solution)/shard_map/ppermute | solution.py:401
  83.0 5.2 %collective-permute-done.4 = f32[48,1024]{1,0:T(8,128)S(1)} collective-permute-done((f32[48,1024]{1,0:T(8,128)S(1)}, f32[48,1024]{1,0:T(8,128)S(1)}, u32[]{:S(2)}, u32[]{:S(2)}) %collective-permute-start.4) | collective-permute-done | bytes 196640 | tf_op jit(solution)/shard_map/ppermute | solution.py:401
  89.0 1.0 collective-permute-start.10
  90.6 0.7 fusion.2
  93.0 1.2 collective-permute-done.12
  95.3 1.2 collective-permute-done.14
  97.5 1.2 collective-permute-done.16
  99.7 1.2 collective-permute-done.18
  101.9 1.2 collective-permute-done.20
  103.0 1.3 collective-permute-start.21
  104.3 67.1 %collective-permute-done.21 = f32[48,1024]{1,0:T(8,128)S(1)} collective-permute-done((f32[48,1024]{1,0:T(8,128)}, f32[48,1024]{1,0:T(8,128)S(1)}, u32[]{:S(2)}, u32[]{:S(2)}) %collective-permute-start.21) | collective-permute-done | bytes 196640 | tf_op jit(solution)/shard_map/ppermute | solution.py:415
  171.4 0.9 collective-permute-start.22
  172.3 1.1 collective-permute-done.22
  173.4 7.1 %conditional.13 = (f32[1,48,512]{2,1,0:T(8,128)}) conditional(s32[]{:T(128)} %convert_element_type.47, f32[48,512]{1,0:T(8,128)} %get-tuple-element.516, (s32[2]{0:T(128)S(1)}, s32[2]{0:T(128)S(1)}, f32[48,1024]{1,0:T(8,128)S(1)}, f32[48,1024]{1,0:T(8,128)S(1)}, f32[48,1024]{1,0:T(8,128)S(1)}, /*index=5*/f32[48,1024]{1,0:T(8,128)S(1)}, ...), branch_computations={%region_13.14_spmd, %region_14.15_spmd} | conditional | bytes 776 | solution.py:421
  173.6 6.9 %links.13 = (f32[48,1024]{1,0:T(8,128)}, f32[48,512]{1,0:T(8,128)}) custom-call(s32[2]{0:T(128)S(1)} %get-tuple-element.460.refs_0_, s32[2]{0:T(128)S(1)} %get-tuple-element.461.refs_1_, f32[48,1024]{1,0:T(8,128)S(1)} %get-tuple-element.462.refs_2_, f32[48,1024]{1,0:T(8,128)S(1)} %get-tuple-element.463.refs_3_, f32[48,1024]{1,0:T(8,128)S(1)} %get-tuple-element.464.refs_4_, ...), custom_call_target="tpu_custom_call" | custom-call | tf_op jit(solution)/shard_map/cond/branch_1_fun/links/pallas_call | solution.py:347
  (68 shorter events, 9.6 us)
Async XLA Ops:
  1.9 10.4 %collective-permute-start.1 = (f32[144,512]{1,0:T(8,128)S(1)}, f32[144,512]{1,0:T(8,128)S(1)}, u32[]{:S(2)}, u32[]{:S(2)}) collective-permute-start(f32[144,512]{1,0:T(8,128)S(1)} %constant_dynamic-update-slice_fusion.own), channel_id=1, source_target_pairs={{18,0},{3,1},{0,2},{17,3},{22,4},{7,5},{4,6},{21,7},{26,8},{11,9},... | collective-permute-start | bytes 884744 | tf_op jit(solution)/shard_map/ppermute | solution.py:380
  2.1 11.0 %collective-permute-start = (f32[144,512]{1,0:T(8,128)S(1)}, f32[144,512]{1,0:T(8,128)S(1)}, u32[]{:S(2)}, u32[]{:S(2)}) collective-permute-start(f32[144,512]{1,0:T(8,128)S(1)} %constant_dynamic-update-slice_fusion.own), channel_id=1, source_target_pairs={{0,1},{1,0},{2,3},{3,2},{4,5},{5,4},{6,7},{7,6},{8,9},{9,8},{10,11... | collective-permute-start | bytes 884744 | tf_op jit(solution)/shard_map/ppermute | solution.py:381
  12.3 1.7 collective-permute-start.2
  71.9 11.1 %collective-permute-start.3 = (f32[48,1024]{1,0:T(8,128)S(1)}, f32[48,1024]{1,0:T(8,128)S(1)}, u32[]{:S(2)}, u32[]{:S(2)}) collective-permute-start(f32[48,1024]{1,0:T(8,128)S(1)} %get-tuple-element.503), channel_id=1, source_target_pairs={{12,0},{0,4},{4,8},{8,12},{28,16},{16,20},{20,24},{24,28},{44,32},... | collective-permute-start | bytes 589832 | tf_op jit(solution)/shard_map/ppermute | solution.py:401
  74.3 13.9 %collective-permute-start.4 = (f32[48,1024]{1,0:T(8,128)S(1)}, f32[48,1024]{1,0:T(8,128)S(1)}, u32[]{:S(2)}, u32[]{:S(2)}) collective-permute-start(f32[48,1024]{1,0:T(8,128)S(1)} %get-tuple-element.503), channel_id=1, source_target_pairs={{8,0},{12,4},{0,8},{4,12},{24,16},{28,20},{16,24},{20,28},{40,32},... | collective-permute-start | bytes 589832 | tf_op jit(solution)/shard_map/ppermute | solution.py:401
  79.1 9.1 %collective-permute-start.5 = (f32[48,1024]{1,0:T(8,128)S(1)}, f32[48,1024]{1,0:T(8,128)S(1)}, u32[]{:S(2)}, u32[]{:S(2)}) collective-permute-start(f32[48,1024]{1,0:T(8,128)S(1)} %get-tuple-element.503), channel_id=1, source_target_pairs={{4,0},{8,4},{12,8},{0,12},{20,16},{24,20},{28,24},{16,28},{36,32},... | collective-permute-start | bytes 589832 | tf_op jit(solution)/shard_map/ppermute | solution.py:401
  88.2 2.3 %copy-start.1 = (f32[48,1024]{1,0:T(8,128)}, f32[48,1024]{1,0:T(8,128)S(1)}, u32[]{:S(2)}) copy-start(f32[48,1024]{1,0:T(8,128)S(1)} %select_select_fusion) | copy-start | bytes 589828
  88.2 2.3 %collective-permute-start.6 = (f32[48,1024]{1,0:T(8,128)S(1)}, f32[48,1024]{1,0:T(8,128)S(1)}, u32[]{:S(2)}, u32[]{:S(2)}) collective-permute-start(f32[48,1024]{1,0:T(8,128)S(1)} %select_select_fusion), channel_id=1, source_target_pairs={{0,16},{4,20},{8,24},{12,28},{1,17},{5,21},{9,25},{13,29},{2,18},{... | collective-permute-start | bytes 589832 | tf_op jit(solution)/shard_map/ppermute | solution.py:415
  89.0 2.3 %collective-permute-start.10 = (f32[48,1024]{1,0:T(8,128)S(1)}, f32[48,1024]{1,0:T(8,128)S(1)}, u32[]{:S(2)}, u32[]{:S(2)}) collective-permute-start(f32[48,1024]{1,0:T(8,128)S(1)} %collective-permute-done.3), channel_id=1, source_target_pairs={{0,1},{1,0},{2,3},{3,2},{4,5},{5,4},{6,7},{7,6},{8,9},{9,8},{10,11... | collective-permute-start | bytes 589832 | tf_op jit(solution)/shard_map/ppermute | solution.py:402
  90.0 1.4 collective-permute-start.8
  90.1 1.6 collective-permute-start.9
  90.5 1.5 collective-permute-start.7
  92.0 0.7 collective-permute-start.11
  92.7 1.5 collective-permute-start.12
  94.2 0.7 collective-permute-start.13
  94.9 1.5 collective-permute-start.14
  96.4 0.7 collective-permute-start.15
  97.1 1.5 collective-permute-start.16
  98.6 0.7 collective-permute-start.17
  99.3 1.5 collective-permute-start.18
  100.8 0.7 collective-permute-start.19
  101.5 1.5 collective-permute-start.20
  103.0 68.4 %collective-permute-start.21 = (f32[48,1024]{1,0:T(8,128)}, f32[48,1024]{1,0:T(8,128)S(1)}, u32[]{:S(2)}, u32[]{:S(2)}) collective-permute-start(f32[48,1024]{1,0:T(8,128)} %get-tuple-element.517), channel_id=1, source_target_pairs={{96,112},{100,116},{104,120},{108,124},{97,113},{101,117},{105,121... | collective-permute-start | bytes 589832 | tf_op jit(solution)/shard_map/ppermute | solution.py:415
  171.4 2.0 %collective-permute-start.22 = (f32[48,1024]{1,0:T(8,128)S(1)}, f32[48,1024]{1,0:T(8,128)S(1)}, u32[]{:S(2)}, u32[]{:S(2)}) collective-permute-start(f32[48,1024]{1,0:T(8,128)S(1)} %collective-permute-done.21), channel_id=1, source_target_pairs={{0,1},{1,0},{2,3},{3,2},{4,5},{5,4},{6,7},{7,6},{8,9},{9,8},{10,11... | collective-permute-start | bytes 589832 | tf_op jit(solution)/shard_map/ppermute | solution.py:416
  (7 other events, 6.9 us)

commit v2 on v1

v2 whole, which is shorter than its diff:
```python
import functools

import jax
import jax.numpy as jnp
from jax import lax
from jax.experimental import pallas as pl
from jax.experimental.pallas import tpu as pltpu
from jax.sharding import PartitionSpec as P

COLS = 128
FACTOR = 4
NEWTON = 2
ROWS = 16
CELLS = 2048
S = 48
TILE = 256
CENTRE = 0.4
ENOUGH = 2.5e-4

VMEM = pl.BlockSpec(memory_space=pltpu.VMEM)
ANY = pl.BlockSpec(memory_space=pl.ANY)
TILES = [slice(start, start + TILE) for start in range(0, CELLS, TILE)]
SMEM = pl.BlockSpec(memory_space=pltpu.SMEM)
PARAMS = pltpu.CompilerParams(vmem_limit_bytes=48 << 20)


def halves(value):
    high = value.astype(jnp.bfloat16)
    low = (value - high.astype(jnp.float32)).astype(jnp.bfloat16)
    return high, low


def stacked(value):
    high, low = halves(value)
    return jnp.concatenate([high, low, high], axis=0)


def wide(matrix):
    rounded = lax.reduce_precision(matrix, 8, 7)
    high, low = rounded.astype(jnp.bfloat16), (matrix - rounded).astype(jnp.bfloat16)
    return jnp.concatenate([high, high, low], axis=1)


def times(matrix, value):
    return jnp.dot(matrix, stacked(value), preferred_element_type=jnp.float32)


def invert_kernel(matrix_ref, out_ref, first_mode, second_mode):
    lane = lax.broadcasted_iota(jnp.int32, (S, COLS), 1)
    row_number = lax.broadcasted_iota(jnp.int32, (S, COLS), 0)
    lane_row = lax.broadcasted_iota(jnp.int32, (1, COLS), 1)
    out_ref[...] = matrix_ref[...]

    def eliminate(k, _):
        current = out_ref[...]
        row = out_ref[pl.ds(k, 1), :]
        first = jnp.sum(jnp.where(lane == k, current, 0.0), axis=1, keepdims=True)
        second = jnp.sum(jnp.where(lane == k + 64, current, 0.0), axis=1, keepdims=True)
        pivot_first = jnp.sum(jnp.where(lane_row == k, row, 0.0), axis=1, keepdims=True)
        pivot_second = jnp.sum(jnp.where(lane_row == k + 64, row, 0.0), axis=1, keepdims=True)
        column = jnp.where(lane < 64, first, second)
        pivot = jnp.where(lane_row < 64, pivot_first, pivot_second)
        at_row = (lane_row == k) | (lane_row == k + 64)
        scaled = jnp.where(at_row, 1.0, row) / pivot
        weights = jnp.where(row_number == k, 0.0, column)
        cleared = jnp.where((lane == k) | (lane == k + 64), 0.0, current)
        updated = cleared - weights * scaled
        out_ref[...] = jnp.where(row_number == k, scaled, updated)
        return 0

    lax.fori_loop(0, S, eliminate, 0)
    for at, mode in ((0, first_mode), (64, second_mode)):
        power = out_ref[:, at : at + S]
        for _ in range(2):
            power = jnp.dot(power, power, precision=lax.Precision.HIGHEST, preferred_element_type=jnp.float32)
        mode[...] = jnp.sum(power, axis=1, keepdims=True)


def invert_pair(first, second):
    gap = jnp.zeros((S, 16), jnp.float32)
    pair = jnp.concatenate([first, gap, second, gap], axis=1)
    pair = pair + jnp.where(jnp.arange(COLS) % 64 >= S, 1.0, 0.0)[None, :]
    column = jax.ShapeDtypeStruct((S, 1), jnp.float32)
    inverted, first_mode, second_mode = pl.pallas_call(
        invert_kernel,
        out_shape=[jax.ShapeDtypeStruct((S, COLS), jnp.float32), column, column],
        in_specs=[VMEM],
        out_specs=[VMEM] * 3,
        name="invert_pair",
    )(pair)
    return inverted[:, :S], inverted[:, 64 : 64 + S], first_mode, second_mode


class Solver:
    def __init__(self, inverse, mode, balance, shift, turns, early):
        self.inverse, self.balance, self.shift = inverse, balance, shift
        self.turns, self.early = turns, early
        self.mode = jnp.broadcast_to(mode[...], (S, TILE))


class Grid:
    def __init__(self, delta, source, spread, saturation, base, change):
        self.delta, self.source = delta, source
        self.spread = jnp.broadcast_to(spread[...], (S, COLS))
        self.saturation = jnp.broadcast_to(saturation[...], (S, COLS))
        self.base, self.change = base, change
        lane = lax.broadcasted_iota(jnp.int32, (S, COLS), 1)
        self.not_first, self.not_last = lane != 0, lane != COLS - 1

    def driven(self, field, r):
        at = slice(r * COLS, (r + 1) * COLS)
        here = field[:, at]
        around = jnp.where(self.not_first, pltpu.roll(here, 1, 1), 0.0) + jnp.where(
            self.not_last, pltpu.roll(here, COLS - 1, 1), 0.0
        )
        if r > 0:
            around = around + field[:, (r - 1) * COLS : r * COLS]
        if r < ROWS - 1:
            around = around + field[:, (r + 1) * COLS : (r + 2) * COLS]
        saturated = self.saturation * (here / (1.0 + here * here) - here)
        return self.spread * around + self.delta[:, at] * here + saturated + self.source[:, at]

    def share(self, solver, at, left):
        return solver.mode * (jnp.sum(left, axis=0, keepdims=True) * solver.balance[:, at])

    def first_turn(self, solver, field, previous, at):
        r = at.start // COLS
        here = field[:, at]
        value = jnp.concatenate([self.driven(field, r + k) for k in range(2)], axis=1)
        value = value + (solver.shift * here if previous is None else previous[:, at])
        base = times(solver.inverse[...], value) - here
        if solver.early:
            return base, base + self.share(solver, at, self.delta[:, at] * base)
        return base, base

    def next_turn(self, solver, at, base, before):
        change = base + times(solver.inverse[...], self.delta[:, at] * before)
        left = self.delta[:, at] * (change - before)
        return change + self.share(solver, at, left), left

    def solve(self, solver, field, previous, level, finish):
        def first(at):
            return self.first_turn(solver, field, previous, at)

        def last(at, base, change):
            finish(at, *self.next_turn(solver, at, base, change))

        def middle(at):
            return self.next_turn(solver, at, self.base[:, at], self.change[:, at])[0]

        if solver.turns == 2:

            @pl.when(level == 0)
            def _():
                for at in TILES:
                    last(at, *first(at))

            @pl.when(level > 0)
            def _():
                for at in TILES:
                    self.base[:, at], self.change[:, at] = first(at)

                def again(_, carry):
                    for at in TILES:
                        self.change[:, at] = middle(at)
                    return carry

                lax.fori_loop(2, 2 << level, again, 0)
                for at in TILES:
                    last(at, self.base[:, at], self.change[:, at])

        else:
            for at in TILES:
                self.base[:, at], self.change[:, at] = first(at)

            @pl.when(level == 0)
            def _():
                for at in TILES:
                    last(at, self.base[:, at], middle(at))

            @pl.when(level > 0)
            def _():
                def pair(_, carry):
                    for at in TILES:
                        change, left = self.next_turn(solver, at, self.base[:, at], middle(at))
                        self.change[:, at] = change
                        finish(at, change, left)
                    return carry

                lax.fori_loop(0, (1 << level) + (1 << level) // 2, pair, 0)

    def fine_steps(self, solver, field, middle, level):
        def first(at, change, _):
            middle[:, at] = field[:, at] + change

        def second(at, change, _):
            field[:, at] = middle[:, at] + change

        def step(_, carry):
            self.solve(solver, field, None, level, first)
            self.solve(solver, middle, field, level, second)
            return carry

        lax.fori_loop(0, FACTOR, step, 0)


def main_kernel(
    where, own, beside, across, corner, fine, coarse, fine_mode, coarse_mode,
    spread, saturation,
    half, rest, mine, delta, source, balance, counts,
    field, middle, keep, base, change, errors, squares, fine_balance,
):
    interval, strip = where[0], where[1]
    width = own.shape[1]
    pieces = (own, beside, across, corner)

    def place(k):
        return pl.ds(pl.multiple_of(jnp.bitwise_xor(strip, k) * width, COLS), width)

    for k, piece in enumerate(pieces):
        decay = piece[S : 2 * S, :]
        delta[:, place(k)] = CENTRE - decay
        source[:, place(k)] = piece[2 * S : 3 * S, :]
        for mode, shift, total in ((fine_mode, 1.0, fine_balance), (coarse_mode, 1.0 / FACTOR, balance)):
            losses = (shift + 4.0 * spread[...] + decay) * mode[...]
            total[:, place(k)] = 1.0 / jnp.sum(losses, axis=0, keepdims=True)
    grid = Grid(delta, source, spread, saturation, base, change)
    fine_solver = Solver(fine, fine_mode, fine_balance, 1.0, 2, False)
    coarse_solver = Solver(coarse, coarse_mode, balance, 1.0 / FACTOR, 3, True)

    def keep_own(condition):
        @pl.when(condition)
        def _():
            mine[...] = field[:, pl.ds(pl.multiple_of(strip * width, COLS), width)]

    def attempt(state):
        level = state[0]
        counts[0] = level
        for k, piece in enumerate(pieces):
            field[:, place(k)] = piece[0:S, :]
        keep_own(interval == 0)

        def interval_steps(phase, carry):
            for at in TILES:
                keep[:, at] = field[:, at]
            grid.fine_steps(fine_solver, field, middle, level)
            keep_own(interval == phase + 1)
            return carry

        lax.fori_loop(0, 2, interval_steps, 0)

        def defect(at, moved, left):
            here = field[:, at]
            middle[:, at] = here - keep[:, at] - moved
            errors[:, at] = left * left
            squares[:, at] = here * here

        grid.solve(coarse_solver, keep, None, level, defect)
        return level + 1, jnp.sum(errors[...]) <= (ENOUGH * ENOUGH) * jnp.sum(squares[...])

    lax.while_loop(lambda state: jnp.logical_not(state[1]) & (state[0] < 6), attempt, (jnp.int32(0), False))
    level = counts[0]

    @pl.when(interval <= 3)
    def _():
        for at in TILES:
            field[:, at] = keep[:, at]

    for at in TILES:
        keep[:, at] = middle[:, at]

    def linked(at, moved, _):
        middle[:, at] = field[:, at] + moved + keep[:, at]

    def link(_, carry):
        grid.solve(coarse_solver, field, None, level, linked)
        for at in TILES:
            field[:, at] = middle[:, at]
        return carry

    lax.fori_loop(4, interval, link, 0)

    def interval_steps(_, carry):
        for at in TILES:
            keep[:, at] = field[:, at]
        grid.fine_steps(fine_solver, field, middle, level)
        return carry

    lax.fori_loop(0, 2, interval_steps, 0)

    def handed(at, moved, _):
        middle[:, at] = field[:, at] - jnp.where(interval <= 4, 0.0, keep[:, at] + moved)

    grid.solve(coarse_solver, keep, None, level, handed)
    keep_own((interval == 3) | (interval == 4))
    half[...] = middle[:, half_at(strip, 0)]
    rest[...] = middle[:, half_at(strip, 1)]


def half_at(strip, other):
    core = jnp.bitwise_xor(jnp.bitwise_and(strip, 1), other)
    return pl.ds(pl.multiple_of(core * (CELLS // 2), COLS), CELLS // 2)


def whole():
    return jax.ShapeDtypeStruct((S, CELLS), jnp.float32)


def half_grid():
    return jax.ShapeDtypeStruct((S, CELLS // 2), jnp.float32)


def line():
    return jax.ShapeDtypeStruct((1, CELLS), jnp.float32)


def scratch(count):
    return [pltpu.VMEM((S, CELLS), jnp.float32) for _ in range(count)]


def run_main(where, pieces, *shared):
    width = pieces[0].shape[1]
    return pl.pallas_call(
        main_kernel,
        out_shape=[
            half_grid(), half_grid(), jax.ShapeDtypeStruct((S, width), jnp.float32),
            whole(), whole(), line(), jax.ShapeDtypeStruct((1,), jnp.int32),
        ],
        in_specs=[SMEM] + [VMEM] * 10,
        out_specs=[VMEM] * 6 + [SMEM],
        scratch_shapes=scratch(7) + [pltpu.VMEM((1, CELLS), jnp.float32)],
        compiler_params=PARAMS,
        name="to_payload",
    )(where, *pieces, *shared)


def slot_of(member, core, j):
    near = jnp.bitwise_xor(member, jnp.where(core == 0, (0, 1, 3, 2)[j % 4], (0, 3, 1, 2)[j % 4]))
    return jnp.bitwise_xor(near, j // 4 * 4)


def chain_kernel(length, seeded, *refs):
    where, counts = refs[:2]
    arrived, payloads = refs[2:4], refs[4 : 4 + 2 * length]
    rest = refs[4 + 2 * length :]
    coefficients = rest[:2]
    coarse, mode, balance, spread, saturation = rest[2:7]
    half, mine, field, middle, base, change, delta, source, stage, fetched, passed = rest[7:]
    member, strip = where[0] % length, where[1]
    width = mine.shape[1]

    def held(piece, slot, k):
        return pltpu.make_async_copy(piece, stage.at[slot, :, half_at(strip, k)], passed.at[slot, k])

    copies = [] if seeded else [pltpu.make_async_copy(arrived[k], field.at[:, half_at(strip, k)], fetched.at[k]) for k in range(2)]
    copies += [
        pltpu.make_async_copy(source_ref, target, fetched.at[2 + k])
        for k, (source_ref, target) in enumerate(zip(coefficients, (delta, source)))
    ]
    for copy in copies:
        copy.start()
    for j in range(length):
        for k in range(2):
            core = jnp.bitwise_xor(jnp.bitwise_and(strip, 1), k)
            held(payloads[2 * j + k], slot_of(member, core, j), k).start()
    for copy in copies:
        copy.wait()
    grid = Grid(delta, source, spread, saturation, base, change)
    solver = Solver(coarse, mode, balance, 1.0 / FACTOR, 3, True)

    def show(slot, state):
        @pl.when(member == slot)
        def _():
            mine[...] = state[:, pl.ds(pl.multiple_of(strip * width, COLS), width)]

    def fetched_payload(slot):
        for k in range(2):
            held(payloads[k], slot, k).wait()

    def link(slot, carry):
        fetched_payload(slot)

        def linked(at, moved, _):
            middle[:, at] = field[:, at] + moved + stage[slot, :, at]

        grid.solve(solver, field, None, counts[0], linked)
        for at in TILES:
            field[:, at] = middle[:, at]
        show(slot, field)
        return carry

    if seeded:
        fetched_payload(0)
        field[...] = stage[0]
        show(0, field)
    lax.fori_loop(1 if seeded else 0, length, link, 0)
    half[...] = field[:, half_at(strip, 0)]


def run_chain(where, counts, arrived, payloads, coefficients, shared):
    length, seeded = len(payloads) // 2, arrived is None
    arrived = payloads[:2] if seeded else arrived
    return pl.pallas_call(
        functools.partial(chain_kernel, length, seeded),
        out_shape=[half_grid(), jax.ShapeDtypeStruct((S, CELLS // 4), jnp.float32)],
        in_specs=[SMEM, SMEM] + [ANY] * (2 + 2 * length + 2) + [VMEM] * 5,
        out_specs=[VMEM, VMEM],
        scratch_shapes=scratch(6)
        + [
            pltpu.VMEM((length, S, CELLS), jnp.float32),
            pltpu.SemaphoreType.DMA((4,)),
            pltpu.SemaphoreType.DMA((length, 2)),
        ],
        compiler_params=PARAMS,
        name=f"links_{length - seeded}",
    )(where, counts, *arrived, *payloads, *coefficients, *shared)


def neighbour_route():
    route = []
    for tm in range(32):
        for strip in range(4):
            high, low, core = (tm // 4) % 2, strip // 2, strip % 2
            y = high * 2 + low
            from_y = (y + 1) % 4 if core else (y - 1) % 4
            from_tm = tm + ((from_y // 2) - high) * 4
            route.append((from_tm * 4 + (from_y % 2) * 2 + core, tm * 4 + strip))
    return route


def per_device(initial_field, decay_rates, source, diffusion, saturation, conversion):
    strip, interval = lax.axis_index("space"), lax.axis_index("tm")
    where = jnp.stack([interval, strip]).astype(jnp.int32)
    own = jnp.concatenate([initial_field, decay_rates, source], axis=0)
    swap = [(0, 1), (1, 0), (2, 3), (3, 2)]
    across = lax.ppermute(own, ("tm", "space"), neighbour_route())
    beside = lax.ppermute(own, "space", swap)
    corner = lax.ppermute(across, "space", swap)

    off_diagonal = conversion * (1.0 - jnp.eye(S, dtype=jnp.float32))
    outflow = jnp.sum(off_diagonal, axis=0)
    still = 4.0 * diffusion + outflow
    centre = jnp.eye(S, dtype=jnp.float32) * (still + CENTRE)[:, None] - off_diagonal
    fine, coarse, fine_mode, coarse_mode = invert_pair(
        centre + jnp.eye(S, dtype=jnp.float32), centre + jnp.eye(S, dtype=jnp.float32) / FACTOR
    )
    fine, coarse = wide(fine), wide(coarse)
    spread, saturation = diffusion[:, None], saturation[:, None]
    half, rest, mine, *coefficients, balance, counts = run_main(
        where, (own, beside, across, corner), fine, coarse, fine_mode, coarse_mode, spread, saturation
    )
    shared = (coarse, coarse_mode, balance, spread, saturation)
    def swapped(piece):
        return [piece, lax.ppermute(piece, "space", swap)]

    def exchanged(piece, flips, lowest):
        route = [(4 * (i ^ flips[c % 2]) + c, 4 * i + c) for i in range(lowest, 32) for c in range(4)]
        return lax.ppermute(piece, ("tm", "space"), route)

    def doubled(piece, lowest):
        second = exchanged(piece, (1, 3), lowest)
        return [second, exchanged(piece, (3, 1), lowest), exchanged(second, (3, 1), lowest)]

    near = sum([swapped(piece) for piece in doubled(half, 4)], [half, rest])

    def advance(active, arrived, payloads, last, mine):
        def run():
            return tuple(run_chain(where, counts, arrived, payloads, coefficients, shared))

        return lax.cond(active, run, lambda: (last, mine))

    def hop(last, start, distance, length):
        return lax.ppermute(last, "tm", [(start - distance + m, start + m) for m in range(length)])

    last, mine = advance(interval // 4 == 1, None, near, half, mine)
    behind, last = lax.optimization_barrier((half, last))
    partner = swapped(lax.ppermute(behind, "tm", [(i ^ 4, i) for i in range(16, 32)]))
    payloads = near + partner + sum([swapped(piece) for piece in doubled(partner[0], 16)], [])
    for quarter in (2, 3):
        arrived = swapped(hop(last, 4 * quarter, 4, 4))
        last, mine = advance(interval // 4 == quarter, arrived, near, last, mine)
    arrived = jnp.where(interval // 4 == 4, hop(last, 16, 4, 4), hop(last, 20, 8, 4))
    last, mine = advance(interval // 8 == 2, swapped(arrived), payloads, last, mine)
    arrived = hop(last, 24, 8, 8)
    last, mine = advance(interval // 8 == 3, swapped(arrived), payloads, last, mine)
    return mine[None]


def solution(mesh):
    in_specs = (P(None, "space"), P(None, "space"), P(None, "space"), P(), P(), P())
    out_specs = P("tm", None, "space")
    return jax.shard_map(
        per_device, mesh=mesh, in_specs=in_specs, out_specs=out_specs, check_vma=False
    )
```

time: 181 us -> 152 us (0.84)
  the two profiles are of different devices: /device:TPU:113 before, /device:TPU:97 now
where the time goes in v2:
time: 152 us; the launch traced here: 151 us
  Pallas kernels  65.7 us (43%)
  starting transfers between devices  50.9 us (33%)
  waiting for transfers between devices  26.7 us (18%)
  local copies, waits for them, and re-layouts  4.17 us (3%)
  other arithmetic  2.71 us (2%)
    pallas_call x1, Pallas kernels, run_main(): pl.pallas_call(main_kernel, out_shape=[half_grid(), half_grid(), jax.Shap...  47.6 us
    ppermute x6, starting transfers between devices, exchanged(): return lax.ppermute(piece, ('tm', 'space'), route)  21.2 us
    ppermute x5, waiting for transfers between devices, hop(): lax.ppermute(last, 'tm', [(start - distance + m, start + m) for m in rang...  15.2 us
    ppermute x11, starting transfers between devices, swapped(): return [piece, lax.ppermute(piece, 'space', swap)]  13.3 us
    pallas_call x1, Pallas kernels, run_chain(): pl.pallas_call(functools.partial(chain_kernel, length, seeded), out_shape...  11.6 us
    ppermute x1, starting transfers between devices, per_device(): lax.ppermute(behind, 'tm', [(i ^ 4, i) for i in range(16, 32)])  7.76 us
    pallas_call x1, Pallas kernels, invert_pair(): pl.pallas_call(invert_kernel, out_shape=[jax.ShapeDtypeStruct((S, COLS),...  6.5 us
    ppermute x5, starting transfers between devices, hop(): lax.ppermute(last, 'tm', [(start - distance + m, start + m) for m in rang...  5.31 us
  transfers between devices with their start and end apart: 26, of which 8 were waited for; matrix products, arithmetic and copies ran while one was open for 2% of the time, Pallas kernels for 4%

profile of v2, /device:TPU:97, one launch (start us, length us, event | category | flops | bytes accessed | tf_op | source)
XLA Modules:
  0.0 150.6 jit_solution(1996748059052607684)
XLA Ops:
  1.9 2.8 %collective-permute-start.1 = (f32[144,512]{1,0:T(8,128)S(1)}, f32[144,512]{1,0:T(8,128)S(1)}, u32[]{:S(2)}, u32[]{:S(2)}) collective-permute-start(f32[144,512]{1,0:T(8,128)S(1)} %constant_dynamic-update-slice_fusion.own), channel_id=1, source_target_pairs={{18,0},{3,1},{0,2},{17,3},{22,4},{7,5},{4,6},{21,7},{26,8},{11,9},... | collective-permute-start | bytes 884744 | tf_op jit(solution)/shard_map/ppermute | solution.py:436
  6.1 6.5 %invert_pair.1 = (f32[48,128]{1,0:T(8,128)}, f32[48,1]{1,0:T(8,128)}, f32[48,1]{1,0:T(8,128)S(1)}) custom-call(f32[48,128]{1,0:T(8,128)} %maximum_add_fusion.matrix_ref), custom_call_target="tpu_custom_call" | custom-call | tf_op jit(solution)/shard_map/invert_pair/pallas_call | solution.py:84
  15.3 47.6 %to_payload.1 = (f32[48,1024]{1,0:T(8,128)S(1)}, f32[48,1024]{1,0:T(8,128)S(1)}, f32[48,512]{1,0:T(8,128)}, f32[48,2048]{1,0:T(8,128)S(1)}, f32[48,2048]{1,0:T(8...) custom-call(s32[2]{0:T(128)S(1)} %pad_add_fusion.where, f32[144,512]{1,0:T(8,128)S(1)} %constant_dynamic-update-slice_fusion.own, ...), custom_call_target="tpu_custom_call" | custom-call | tf_op jit(solution)/shard_map/to_payload/pallas_call | solution.py:323
  62.9 7.8 %collective-permute-start.3 = (f32[48,1024]{1,0:T(8,128)S(1)}, f32[48,1024]{1,0:T(8,128)S(1)}, u32[]{:S(2)}, u32[]{:S(2)}) collective-permute-start(f32[48,1024]{1,0:T(8,128)S(1)} %get-tuple-element.393), channel_id=1, source_target_pairs={{20,16},{29,17},{22,18},{31,19},{16,20},{25,21},{18,22},{27,23},{2... | collective-permute-start | bytes 589832 | tf_op jit(solution)/shard_map/ppermute | solution.py:458
  70.8 1.9 %collective-permute-start.5 = (f32[48,1024]{1,0:T(8,128)S(1)}, f32[48,1024]{1,0:T(8,128)S(1)}, u32[]{:S(2)}, u32[]{:S(2)}) collective-permute-start(f32[48,1024]{1,0:T(8,128)S(1)} %get-tuple-element.393), channel_id=1, source_target_pairs={{28,16},{21,17},{30,18},{23,19},{24,20},{17,21},{26,22},{19,23},{2... | collective-permute-start | bytes 589832 | tf_op jit(solution)/shard_map/ppermute | solution.py:458
  72.7 1.1 collective-permute-done.3
  73.8 2.3 %collective-permute-start.7 = (f32[48,1024]{1,0:T(8,128)S(1)}, f32[48,1024]{1,0:T(8,128)S(1)}, u32[]{:S(2)}, u32[]{:S(2)}) collective-permute-start(f32[48,1024]{1,0:T(8,128)S(1)} %collective-permute-done.3), channel_id=1, source_target_pairs={{28,16},{21,17},{30,18},{23,19},{24,20},{17,21},{26,22},{19,23},{2... | collective-permute-start | bytes 589832 | tf_op jit(solution)/shard_map/ppermute | solution.py:458
  76.1 4.0 %collective-permute-start.4 = (f32[48,1024]{1,0:T(8,128)S(1)}, f32[48,1024]{1,0:T(8,128)S(1)}, u32[]{:S(2)}, u32[]{:S(2)}) collective-permute-start(f32[48,1024]{1,0:T(8,128)S(1)} %collective-permute-done.3), channel_id=1, source_target_pairs={{0,1},{1,0},{2,3},{3,2},{4,5},{5,4},{6,7},{7,6},{8,9},{9,8},{10,11... | collective-permute-start | bytes 589832 | tf_op jit(solution)/shard_map/ppermute | solution.py:454
  80.2 3.4 %collective-permute-start.8 = (f32[48,1024]{1,0:T(8,128)S(1)}, f32[48,1024]{1,0:T(8,128)S(1)}, u32[]{:S(2)}, u32[]{:S(2)}) collective-permute-start(f32[48,1024]{1,0:T(8,128)S(1)} %collective-permute-done.7), channel_id=1, source_target_pairs={{0,1},{1,0},{2,3},{3,2},{4,5},{5,4},{6,7},{7,6},{8,9},{9,8},{10,11... | collective-permute-start | bytes 589832 | tf_op jit(solution)/shard_map/ppermute | solution.py:454
  86.5 7.8 %collective-permute-start.16 = (f32[48,1024]{1,0:T(8,128)S(1)}, f32[48,1024]{1,0:T(8,128)S(1)}, u32[]{:S(2)}, u32[]{:S(2)}) collective-permute-start(f32[48,1024]{1,0:T(8,128)S(1)} %get-tuple-element.393), channel_id=1, source_target_pairs={{80,64},{84,68},{88,72},{92,76},{64,80},{68,84},{72,88},{76,92},{1... | collective-permute-start | bytes 589832 | tf_op jit(solution)/shard_map/ppermute | solution.py:477
  95.0 4.4 %collective-permute-done.16 = f32[48,1024]{1,0:T(8,128)S(1)} collective-permute-done((f32[48,1024]{1,0:T(8,128)S(1)}, f32[48,1024]{1,0:T(8,128)S(1)}, u32[]{:S(2)}, u32[]{:S(2)}) %collective-permute-start.16) | collective-permute-done | bytes 196640 | tf_op jit(solution)/shard_map/ppermute | solution.py:477
  99.4 4.8 %collective-permute-start.18 = (f32[48,1024]{1,0:T(8,128)S(1)}, f32[48,1024]{1,0:T(8,128)S(1)}, u32[]{:S(2)}, u32[]{:S(2)}) collective-permute-start(f32[48,1024]{1,0:T(8,128)S(1)} %collective-permute-done.16), channel_id=1, source_target_pairs={{68,64},{77,65},{70,66},{79,67},{64,68},{73,69},{66,70},{75,71},{7... | collective-permute-start | bytes 589832 | tf_op jit(solution)/shard_map/ppermute | solution.py:458
  104.4 1.9 %collective-permute-start.20 = (f32[48,1024]{1,0:T(8,128)S(1)}, f32[48,1024]{1,0:T(8,128)S(1)}, u32[]{:S(2)}, u32[]{:S(2)}) collective-permute-start(f32[48,1024]{1,0:T(8,128)S(1)} %collective-permute-done.16), channel_id=1, source_target_pairs={{76,64},{69,65},{78,66},{71,67},{72,68},{65,69},{74,70},{67,71},{6... | collective-permute-start | bytes 589832 | tf_op jit(solution)/shard_map/ppermute | solution.py:458
  107.3 2.4 %collective-permute-start.22 = (f32[48,1024]{1,0:T(8,128)S(1)}, f32[48,1024]{1,0:T(8,128)S(1)}, u32[]{:S(2)}, u32[]{:S(2)}) collective-permute-start(f32[48,1024]{1,0:T(8,128)S(1)} %collective-permute-done.18), channel_id=1, source_target_pairs={{76,64},{69,65},{78,66},{71,67},{72,68},{65,69},{74,70},{67,71},{6... | collective-permute-start | bytes 589832 | tf_op jit(solution)/shard_map/ppermute | solution.py:458
  109.7 1.4 collective-permute-start.13
  111.1 1.3 collective-permute-start.14
  112.4 3.2 %collective-permute-start.17 = (f32[48,1024]{1,0:T(8,128)S(1)}, f32[48,1024]{1,0:T(8,128)S(1)}, u32[]{:S(2)}, u32[]{:S(2)}) collective-permute-start(f32[48,1024]{1,0:T(8,128)S(1)} %collective-permute-done.16), channel_id=1, source_target_pairs={{0,1},{1,0},{2,3},{3,2},{4,5},{5,4},{6,7},{7,6},{8,9},{9,8},{10,11... | collective-permute-start | bytes 589832 | tf_op jit(solution)/shard_map/ppermute | solution.py:454
  116.5 1.6 %broadcast_select_fusion = f32[48,1024]{1,0:T(8,128)} fusion(f32[48,1024]{1,0:T(8,128)} %collective-permute-done.13, f32[48,1024]{1,0:T(8,128)} %collective-permute-done.14, pred[]{:T(512)S(6)} %eq.38), kind=kLoop, calls=%fused_computation | loop fusion | flops 49152 | bytes 589825 | tf_op jit(solution)/shard_map/jit(_where)/select_n | solution.py:482
  118.7 1.4 collective-permute-done.15
  120.1 1.3 collective-permute-start.24
  121.4 15.2 %collective-permute-done.24 = f32[48,1024]{1,0:T(8,128)} collective-permute-done((f32[48,1024]{1,0:T(8,128)}, f32[48,1024]{1,0:T(8,128)}, u32[]{:S(2)}, u32[]{:S(2)}) %collective-permute-start.24) | collective-permute-done | bytes 196640 | tf_op jit(solution)/shard_map/ppermute | solution.py:473
  137.3 1.4 collective-permute-done.25
  138.7 11.8 %conditional.9 = (f32[1,48,512]{2,1,0:T(8,128)}) conditional(s32[]{:T(128)} %convert_element_type.35, f32[48,512]{1,0:T(8,128)} %get-tuple-element.394, (s32[2]{0:T(128)S(1)}, s32[1]{0:T(128)}, f32[48,1024]{1,0:T(8,128)}, f32[48,1024]{1,0:T(8,128)}, f32[48,1024]{1,0:T(8,128)S(1)}, /*index=5*/f32[48,1024]{1,0:T(8,128)S(1)}, ...), branch_computations={%region_9.10_spmd, %region_10.11_spmd} | conditional | bytes 776 | solution.py:470
  138.9 11.6 %links_8.3 = (f32[48,1024]{1,0:T(8,128)}, f32[48,512]{1,0:T(8,128)}) custom-call(s32[2]{0:T(128)S(1)} %get-tuple-element.332.refs_0_, s32[1]{0:T(128)} %get-tuple-element.333.refs_1_, f32[48,1024]{1,0:T(8,128)} %get-tuple-element.334.refs_2_, f32[48,1024]{1,0:T(8,128)} %get-tuple-element.335.refs_3_, f32[48,1024]{1,0:T(8,128)S(1)} %get-tuple-element.336.refs_4_, ...), custom_call_target="tpu_custom_call" | custom-call | tf_op jit(solution)/shard_map/cond/branch_1_fun/links_8/pallas_call | solution.py:403
  (72 shorter events, 13.7 us)
Async XLA Ops:
  1.9 11.7 %collective-permute-start.1 = (f32[144,512]{1,0:T(8,128)S(1)}, f32[144,512]{1,0:T(8,128)S(1)}, u32[]{:S(2)}, u32[]{:S(2)}) collective-permute-start(f32[144,512]{1,0:T(8,128)S(1)} %constant_dynamic-update-slice_fusion.own), channel_id=1, source_target_pairs={{18,0},{3,1},{0,2},{17,3},{22,4},{7,5},{4,6},{21,7},{26,8},{11,9},... | collective-permute-start | bytes 884744 | tf_op jit(solution)/shard_map/ppermute | solution.py:436
  4.7 9.6 %collective-permute-start = (f32[144,512]{1,0:T(8,128)S(1)}, f32[144,512]{1,0:T(8,128)S(1)}, u32[]{:S(2)}, u32[]{:S(2)}) collective-permute-start(f32[144,512]{1,0:T(8,128)S(1)} %constant_dynamic-update-slice_fusion.own), channel_id=1, source_target_pairs={{0,1},{1,0},{2,3},{3,2},{4,5},{5,4},{6,7},{7,6},{8,9},{9,8},{10,11... | collective-permute-start | bytes 884744 | tf_op jit(solution)/shard_map/ppermute | solution.py:437
  62.9 10.9 %collective-permute-start.3 = (f32[48,1024]{1,0:T(8,128)S(1)}, f32[48,1024]{1,0:T(8,128)S(1)}, u32[]{:S(2)}, u32[]{:S(2)}) collective-permute-start(f32[48,1024]{1,0:T(8,128)S(1)} %get-tuple-element.393), channel_id=1, source_target_pairs={{20,16},{29,17},{22,18},{31,19},{16,20},{25,21},{18,22},{27,23},{2... | collective-permute-start | bytes 589832 | tf_op jit(solution)/shard_map/ppermute | solution.py:458
  70.8 9.3 %collective-permute-start.5 = (f32[48,1024]{1,0:T(8,128)S(1)}, f32[48,1024]{1,0:T(8,128)S(1)}, u32[]{:S(2)}, u32[]{:S(2)}) collective-permute-start(f32[48,1024]{1,0:T(8,128)S(1)} %get-tuple-element.393), channel_id=1, source_target_pairs={{28,16},{21,17},{30,18},{23,19},{24,20},{17,21},{26,22},{19,23},{2... | collective-permute-start | bytes 589832 | tf_op jit(solution)/shard_map/ppermute | solution.py:458
  73.8 6.4 %collective-permute-start.7 = (f32[48,1024]{1,0:T(8,128)S(1)}, f32[48,1024]{1,0:T(8,128)S(1)}, u32[]{:S(2)}, u32[]{:S(2)}) collective-permute-start(f32[48,1024]{1,0:T(8,128)S(1)} %collective-permute-done.3), channel_id=1, source_target_pairs={{28,16},{21,17},{30,18},{23,19},{24,20},{17,21},{26,22},{19,23},{2... | collective-permute-start | bytes 589832 | tf_op jit(solution)/shard_map/ppermute | solution.py:458
  76.1 7.5 %collective-permute-start.4 = (f32[48,1024]{1,0:T(8,128)S(1)}, f32[48,1024]{1,0:T(8,128)S(1)}, u32[]{:S(2)}, u32[]{:S(2)}) collective-permute-start(f32[48,1024]{1,0:T(8,128)S(1)} %collective-permute-done.3), channel_id=1, source_target_pairs={{0,1},{1,0},{2,3},{3,2},{4,5},{5,4},{6,7},{7,6},{8,9},{9,8},{10,11... | collective-permute-start | bytes 589832 | tf_op jit(solution)/shard_map/ppermute | solution.py:454
  80.1 3.6 %collective-permute-start.6 = (f32[48,1024]{1,0:T(8,128)S(1)}, f32[48,1024]{1,0:T(8,128)S(1)}, u32[]{:S(2)}, u32[]{:S(2)}) collective-permute-start(f32[48,1024]{1,0:T(8,128)S(1)} %collective-permute-done.5), channel_id=1, source_target_pairs={{0,1},{1,0},{2,3},{3,2},{4,5},{5,4},{6,7},{7,6},{8,9},{9,8},{10,11... | collective-permute-start | bytes 589832 | tf_op jit(solution)/shard_map/ppermute | solution.py:454
  80.2 4.5 %collective-permute-start.8 = (f32[48,1024]{1,0:T(8,128)S(1)}, f32[48,1024]{1,0:T(8,128)S(1)}, u32[]{:S(2)}, u32[]{:S(2)}) collective-permute-start(f32[48,1024]{1,0:T(8,128)S(1)} %collective-permute-done.7), channel_id=1, source_target_pairs={{0,1},{1,0},{2,3},{3,2},{4,5},{5,4},{6,7},{7,6},{8,9},{9,8},{10,11... | collective-permute-start | bytes 589832 | tf_op jit(solution)/shard_map/ppermute | solution.py:454
  86.1 8.2 %collective-permute-start.10 = (f32[48,1024]{1,0:T(8,128)S(1)}, f32[48,1024]{1,0:T(8,128)S(1)}, u32[]{:S(2)}, u32[]{:S(2)}) collective-permute-start(f32[48,1024]{1,0:T(8,128)S(1)} %collective-permute-done.9), channel_id=1, source_target_pairs={{0,1},{1,0},{2,3},{3,2},{4,5},{5,4},{6,7},{7,6},{8,9},{9,8},{10,11... | collective-permute-start | bytes 589832 | tf_op jit(solution)/shard_map/ppermute | solution.py:454
  86.5 12.9 %collective-permute-start.16 = (f32[48,1024]{1,0:T(8,128)S(1)}, f32[48,1024]{1,0:T(8,128)S(1)}, u32[]{:S(2)}, u32[]{:S(2)}) collective-permute-start(f32[48,1024]{1,0:T(8,128)S(1)} %get-tuple-element.393), channel_id=1, source_target_pairs={{80,64},{84,68},{88,72},{92,76},{64,80},{68,84},{72,88},{76,92},{1... | collective-permute-start | bytes 589832 | tf_op jit(solution)/shard_map/ppermute | solution.py:477
  94.3 9.9 %collective-permute-start.11 = (f32[48,1024]{1,0:T(8,128)}, f32[48,1024]{1,0:T(8,128)S(1)}, u32[]{:S(2)}, u32[]{:S(2)}) collective-permute-start(f32[48,1024]{1,0:T(8,128)} %get-tuple-element.391), channel_id=1, source_target_pairs={{32,48},{36,52},{40,56},{44,60},{33,49},{37,53},{41,57},{45,61},{3... | collective-permute-start | bytes 589832 | tf_op jit(solution)/shard_map/ppermute | solution.py:473
  99.4 7.9 %collective-permute-start.18 = (f32[48,1024]{1,0:T(8,128)S(1)}, f32[48,1024]{1,0:T(8,128)S(1)}, u32[]{:S(2)}, u32[]{:S(2)}) collective-permute-start(f32[48,1024]{1,0:T(8,128)S(1)} %collective-permute-done.16), channel_id=1, source_target_pairs={{68,64},{77,65},{70,66},{79,67},{64,68},{73,69},{66,70},{75,71},{7... | collective-permute-start | bytes 589832 | tf_op jit(solution)/shard_map/ppermute | solution.py:458
  104.3 5.4 %collective-permute-start.12 = (f32[48,1024]{1,0:T(8,128)S(1)}, f32[48,1024]{1,0:T(8,128)}, u32[]{:S(2)}, u32[]{:S(2)}) collective-permute-start(f32[48,1024]{1,0:T(8,128)S(1)} %collective-permute-done.11), channel_id=1, source_target_pairs={{0,1},{1,0},{2,3},{3,2},{4,5},{5,4},{6,7},{7,6},{8,9},{9,8},{10,11... | collective-permute-start | bytes 589832 | tf_op jit(solution)/shard_map/ppermute | solution.py:454
  104.4 11.2 %collective-permute-start.20 = (f32[48,1024]{1,0:T(8,128)S(1)}, f32[48,1024]{1,0:T(8,128)S(1)}, u32[]{:S(2)}, u32[]{:S(2)}) collective-permute-start(f32[48,1024]{1,0:T(8,128)S(1)} %collective-permute-done.16), channel_id=1, source_target_pairs={{76,64},{69,65},{78,66},{71,67},{72,68},{65,69},{74,70},{67,71},{6... | collective-permute-start | bytes 589832 | tf_op jit(solution)/shard_map/ppermute | solution.py:458
  107.3 8.3 %collective-permute-start.22 = (f32[48,1024]{1,0:T(8,128)S(1)}, f32[48,1024]{1,0:T(8,128)S(1)}, u32[]{:S(2)}, u32[]{:S(2)}) collective-permute-start(f32[48,1024]{1,0:T(8,128)S(1)} %collective-permute-done.18), channel_id=1, source_target_pairs={{76,64},{69,65},{78,66},{71,67},{72,68},{65,69},{74,70},{67,71},{6... | collective-permute-start | bytes 589832 | tf_op jit(solution)/shard_map/ppermute | solution.py:458
  109.7 6.8 %collective-permute-start.13 = (f32[48,1024]{1,0:T(8,128)}, f32[48,1024]{1,0:T(8,128)}, u32[]{:S(2)}, u32[]{:S(2)}) collective-permute-start(f32[48,1024]{1,0:T(8,128)} %get-tuple-element.392), channel_id=1, source_target_pairs={{48,64},{52,68},{56,72},{60,76},{49,65},{53,69},{57,73},{61,77},{5... | collective-permute-start | bytes 589832 | tf_op jit(solution)/shard_map/ppermute | solution.py:473
  111.1 5.5 %collective-permute-start.14 = (f32[48,1024]{1,0:T(8,128)}, f32[48,1024]{1,0:T(8,128)}, u32[]{:S(2)}, u32[]{:S(2)}) collective-permute-start(f32[48,1024]{1,0:T(8,128)} %get-tuple-element.392), channel_id=1, source_target_pairs={{48,80},{52,84},{56,88},{60,92},{49,81},{53,85},{57,89},{61,93},{5... | collective-permute-start | bytes 589832 | tf_op jit(solution)/shard_map/ppermute | solution.py:473
  112.4 6.3 %collective-permute-start.17 = (f32[48,1024]{1,0:T(8,128)S(1)}, f32[48,1024]{1,0:T(8,128)S(1)}, u32[]{:S(2)}, u32[]{:S(2)}) collective-permute-start(f32[48,1024]{1,0:T(8,128)S(1)} %collective-permute-done.16), channel_id=1, source_target_pairs={{0,1},{1,0},{2,3},{3,2},{4,5},{5,4},{6,7},{7,6},{8,9},{9,8},{10,11... | collective-permute-start | bytes 589832 | tf_op jit(solution)/shard_map/ppermute | solution.py:454
  115.6 3.1 %collective-permute-start.19 = (f32[48,1024]{1,0:T(8,128)S(1)}, f32[48,1024]{1,0:T(8,128)}, u32[]{:S(2)}, u32[]{:S(2)}) collective-permute-start(f32[48,1024]{1,0:T(8,128)S(1)} %collective-permute-done.18), channel_id=1, source_target_pairs={{0,1},{1,0},{2,3},{3,2},{4,5},{5,4},{6,7},{7,6},{8,9},{9,8},{10,11... | collective-permute-start | bytes 589832 | tf_op jit(solution)/shard_map/ppermute | solution.py:454
  115.6 3.1 %collective-permute-start.21 = (f32[48,1024]{1,0:T(8,128)S(1)}, f32[48,1024]{1,0:T(8,128)}, u32[]{:S(2)}, u32[]{:S(2)}) collective-permute-start(f32[48,1024]{1,0:T(8,128)S(1)} %collective-permute-done.20), channel_id=1, source_target_pairs={{0,1},{1,0},{2,3},{3,2},{4,5},{5,4},{6,7},{7,6},{8,9},{9,8},{10,11... | collective-permute-start | bytes 589832 | tf_op jit(solution)/shard_map/ppermute | solution.py:454
  116.5 2.2 %collective-permute-start.23 = (f32[48,1024]{1,0:T(8,128)S(1)}, f32[48,1024]{1,0:T(8,128)}, u32[]{:S(2)}, u32[]{:S(2)}) collective-permute-start(f32[48,1024]{1,0:T(8,128)S(1)} %collective-permute-done.22), channel_id=1, source_target_pairs={{0,1},{1,0},{2,3},{3,2},{4,5},{5,4},{6,7},{7,6},{8,9},{9,8},{10,11... | collective-permute-start | bytes 589832 | tf_op jit(solution)/shard_map/ppermute | solution.py:454
  118.2 1.9 %collective-permute-start.15 = (f32[48,1024]{1,0:T(8,128)}, f32[48,1024]{1,0:T(8,128)}, u32[]{:S(2)}, u32[]{:S(2)}) collective-permute-start(f32[48,1024]{1,0:T(8,128)} %broadcast_select_fusion), channel_id=1, source_target_pairs={{0,1},{1,0},{2,3},{3,2},{4,5},{5,4},{6,7},{7,6},{8,9},{9,8},{10,11... | collective-permute-start | bytes 589832 | tf_op jit(solution)/shard_map/ppermute | solution.py:454
  120.1 16.5 %collective-permute-start.24 = (f32[48,1024]{1,0:T(8,128)}, f32[48,1024]{1,0:T(8,128)}, u32[]{:S(2)}, u32[]{:S(2)}) collective-permute-start(f32[48,1024]{1,0:T(8,128)} %get-tuple-element.395), channel_id=1, source_target_pairs={{64,96},{68,100},{72,104},{76,108},{80,112},{84,116},{88,120},{92,... | collective-permute-start | bytes 589832 | tf_op jit(solution)/shard_map/ppermute | solution.py:473
  136.6 2.1 %collective-permute-start.25 = (f32[48,1024]{1,0:T(8,128)}, f32[48,1024]{1,0:T(8,128)}, u32[]{:S(2)}, u32[]{:S(2)}) collective-permute-start(f32[48,1024]{1,0:T(8,128)} %collective-permute-done.24), channel_id=1, source_target_pairs={{0,1},{1,0},{2,3},{3,2},{4,5},{5,4},{6,7},{7,6},{8,9},{9,8},{10,11... | collective-permute-start | bytes 589832 | tf_op jit(solution)/shard_map/ppermute | solution.py:454
  (11 other events, 96.4 us)

commit v3 on v2

--- a/solution.py
+++ b/solution.py
@@ -51,24 +51,38 @@
     lane_row = lax.broadcasted_iota(jnp.int32, (1, COLS), 1)
     out_ref[...] = matrix_ref[...]
 
-    def eliminate(k, _):
+    def taken(values, numbers, number):
+        return jnp.sum(jnp.where(numbers == number, values, 0.0), axis=1, keepdims=True)
+
+    def both(numbers, first, second):
+        return jnp.where(numbers < 64, first, second)
+
+    def eliminate(turn, _):
+        k = 2 * turn
         current = out_ref[...]
-        row = out_ref[pl.ds(k, 1), :]
-        first = jnp.sum(jnp.where(lane == k, current, 0.0), axis=1, keepdims=True)
-        second = jnp.sum(jnp.where(lane == k + 64, current, 0.0), axis=1, keepdims=True)
-        pivot_first = jnp.sum(jnp.where(lane_row == k, row, 0.0), axis=1, keepdims=True)
-        pivot_second = jnp.sum(jnp.where(lane_row == k + 64, row, 0.0), axis=1, keepdims=True)
-        column = jnp.where(lane < 64, first, second)
-        pivot = jnp.where(lane_row < 64, pivot_first, pivot_second)
-        at_row = (lane_row == k) | (lane_row == k + 64)
-        scaled = jnp.where(at_row, 1.0, row) / pivot
-        weights = jnp.where(row_number == k, 0.0, column)
-        cleared = jnp.where((lane == k) | (lane == k + 64), 0.0, current)
-        updated = cleared - weights * scaled
-        out_ref[...] = jnp.where(row_number == k, scaled, updated)
+        rows = [out_ref[pl.ds(k + p, 1), :] for p in range(2)]
+        columns = [
+            both(lane, taken(current, lane, k + p), taken(current, lane, k + 64 + p)) for p in range(2)
+        ]
+        block = [
+            [both(lane_row, taken(row, lane_row, k + p), taken(row, lane_row, k + 64 + p)) for p in range(2)]
+            for row in rows
+        ]
+        scale = 1.0 / (block[0][0] * block[1][1] - block[0][1] * block[1][0])
+        at = [(lane_row == k + p) | (lane_row == k + 64 + p) for p in range(2)]
+        either = at[0] | at[1]
+        freed = [jnp.where(either, jnp.where(at[p], 1.0, 0.0), rows[p]) for p in range(2)]
+        scaled = [
+            scale * (block[1][1] * freed[0] - block[0][1] * freed[1]),
+            scale * (block[0][0] * freed[1] - block[1][0] * freed[0]),
+        ]
+        updated = jnp.where(either, 0.0, current) - columns[0] * scaled[0] - columns[1] * scaled[1]
+        for p in range(2):
+            updated = jnp.where(row_number == k + p, scaled[p], updated)
+        out_ref[...] = updated
         return 0
 
-    lax.fori_loop(0, S, eliminate, 0)
+    lax.fori_loop(0, S // 2, eliminate, 0)
     for at, mode in ((0, first_mode), (64, second_mode)):
         power = out_ref[:, at : at + S]
         for _ in range(2):
@@ -339,10 +353,11 @@
     return jnp.bitwise_xor(near, j // 4 * 4)
 
 
-def chain_kernel(length, seeded, *refs):
+def chain_kernel(length, sources, *refs):
     where, counts = refs[:2]
-    arrived, payloads = refs[2:4], refs[4 : 4 + 2 * length]
-    rest = refs[4 + 2 * length :]
+    arrived, refs = refs[2 : 2 + 2 * sources], refs[2 + 2 * sources :]
+    payloads, rest = refs[: 2 * length], refs[2 * length :]
+    seeded = sources == 0
     coefficients = rest[:2]
     coarse, mode, balance, spread, saturation = rest[2:7]
     half, mine, field, middle, base, change, delta, source, stage, fetched, passed = rest[7:]
@@ -352,8 +367,21 @@
     def held(piece, slot, k):
         return pltpu.make_async_copy(piece, stage.at[slot, :, half_at(strip, k)], passed.at[slot, k])
 
-    copies = [] if seeded else [pltpu.make_async_copy(arrived[k], field.at[:, half_at(strip, k)], fetched.at[k]) for k in range(2)]
-    copies += [
+    def coming(k):
+        return pltpu.make_async_copy(arrived[k], field.at[:, half_at(strip, k % 2)], fetched.at[k % 2])
+
+    if sources > 1:
+        for way in range(sources):
+
+            @pl.when(member // 4 == way)
+            def _():
+                for k in range(2):
+                    coming(2 * way + k).start()
+
+    elif sources > 0:
+        for k in range(2):
+            coming(k).start()
+    copies = [
         pltpu.make_async_copy(source_ref, target, fetched.at[2 + k])
         for k, (source_ref, target) in enumerate(zip(coefficients, (delta, source)))
     ]
@@ -363,7 +391,7 @@
         for k in range(2):
             core = jnp.bitwise_xor(jnp.bitwise_and(strip, 1), k)
             held(payloads[2 * j + k], slot_of(member, core, j), k).start()
-    for copy in copies:
+    for copy in copies + ([] if seeded else [coming(0), coming(1)]):
         copy.wait()
     grid = Grid(delta, source, spread, saturation, base, change)
     solver = Solver(coarse, mode, balance, 1.0 / FACTOR, 3, True)
@@ -398,12 +426,11 @@
 
 
 def run_chain(where, counts, arrived, payloads, coefficients, shared):
-    length, seeded = len(payloads) // 2, arrived is None
-    arrived = payloads[:2] if seeded else arrived
+    length, sources = len(payloads) // 2, len(arrived) // 2
     return pl.pallas_call(
-        functools.partial(chain_kernel, length, seeded),
+        functools.partial(chain_kernel, length, sources),
         out_shape=[half_grid(), jax.ShapeDtypeStruct((S, CELLS // 4), jnp.float32)],
-        in_specs=[SMEM, SMEM] + [ANY] * (2 + 2 * length + 2) + [VMEM] * 5,
+        in_specs=[SMEM, SMEM] + [ANY] * (2 * sources + 2 * length + 2) + [VMEM] * 5,
         out_specs=[VMEM, VMEM],
         scratch_shapes=scratch(6)
         + [
@@ -412,7 +439,7 @@
             pltpu.SemaphoreType.DMA((length, 2)),
         ],
         compiler_params=PARAMS,
-        name=f"links_{length - seeded}",
+        name=f"links_{length}_{sources}",
     )(where, counts, *arrived, *payloads, *coefficients, *shared)
 
 
@@ -472,15 +499,15 @@
     def hop(last, start, distance, length):
         return lax.ppermute(last, "tm", [(start - distance + m, start + m) for m in range(length)])
 
-    last, mine = advance(interval // 4 == 1, None, near, half, mine)
+    last, mine = advance(interval // 4 == 1, [], near, half, mine)
     behind, last = lax.optimization_barrier((half, last))
     partner = swapped(lax.ppermute(behind, "tm", [(i ^ 4, i) for i in range(16, 32)]))
     payloads = near + partner + sum([swapped(piece) for piece in doubled(partner[0], 16)], [])
     for quarter in (2, 3):
         arrived = swapped(hop(last, 4 * quarter, 4, 4))
         last, mine = advance(interval // 4 == quarter, arrived, near, last, mine)
-    arrived = jnp.where(interval // 4 == 4, hop(last, 16, 4, 4), hop(last, 20, 8, 4))
-    last, mine = advance(interval // 8 == 2, swapped(arrived), payloads, last, mine)
+    arrived = swapped(hop(last, 16, 4, 4)) + swapped(hop(last, 20, 8, 4))
+    last, mine = advance(interval // 8 == 2, arrived, payloads, last, mine)
     arrived = hop(last, 24, 8, 8)
     last, mine = advance(interval // 8 == 3, swapped(arrived), payloads, last, mine)
     return mine[None]

time: 152 us -> 150 us (0.987)
  Pallas kernels: 65.7 us -> 63.9 us
    pallas_call x1, Pallas kernels: 6.5 us -> 4.57 us  [invert_pair(): pl.pallas_call(invert_kernel, out_shape=[jax.ShapeDtypeStruct((S, COLS),...]
    select_n x1 -> x0, other arithmetic: 1.64 us -> none  [per_device(): jnp.where(interval // 4 == 4, hop(last, 16, 4, 4), hop(last, 20, 8, 4))]
    ppermute x5, waiting for transfers between devices: 15.2 us -> 16.8 us  [hop(): lax.ppermute(last, 'tm', [(start - distance + m, start + m) for m in rang...]
    ppermute x11 -> x12, starting transfers between devices: 13.3 us -> 12.1 us  [swapped(): return [piece, lax.ppermute(piece, 'space', swap)]]
    unnamed x20 -> x16, local copies, waits for them, and re-layouts: 3.11 us -> 3.46 us
    ppermute x11 -> x12, waiting for transfers between devices: 3.89 us -> 4.04 us  [swapped(): return [piece, lax.ppermute(piece, 'space', swap)]]
  transfers between devices with their start and end apart: 26 -> 27, of which waited for: 8 -> 11; matrix products, arithmetic and copies ran while one was open for 2% -> 1% of each run, Pallas kernels for 4% -> 3%
where the time goes in v3:
time: 150 us; the launch traced here: 149 us
  Pallas kernels  63.9 us (43%)
  starting transfers between devices  52.1 us (35%)
  waiting for transfers between devices  27 us (18%)
  local copies, waits for them, and re-layouts  3.85 us (3%)
  other arithmetic  1.88 us (1%)
    pallas_call x1, Pallas kernels, run_main(): pl.pallas_call(main_kernel, out_shape=[half_grid(), half_grid(), jax.Shap...  47.6 us
    ppermute x6, starting transfers between devices, exchanged(): return lax.ppermute(piece, ('tm', 'space'), route)  21.6 us
    ppermute x5, waiting for transfers between devices, hop(): lax.ppermute(last, 'tm', [(start - distance + m, start + m) for m in rang...  16.8 us
    ppermute x12, starting transfers between devices, swapped(): return [piece, lax.ppermute(piece, 'space', swap)]  12.1 us
    pallas_call x1, Pallas kernels, run_chain(): pl.pallas_call(functools.partial(chain_kernel, length, sources), out_shap...  11.6 us
    ppermute x1, starting transfers between devices, per_device(): lax.ppermute(behind, 'tm', [(i ^ 4, i) for i in range(16, 32)])  8.93 us
    ppermute x5, starting transfers between devices, hop(): lax.ppermute(last, 'tm', [(start - distance + m, start + m) for m in rang...  6.02 us
    pallas_call x1, Pallas kernels, invert_pair(): pl.pallas_call(invert_kernel, out_shape=[jax.ShapeDtypeStruct((S, COLS),...  4.57 us
  transfers between devices with their start and end apart: 27, of which 11 were waited for; matrix products, arithmetic and copies ran while one was open for 1% of the time, Pallas kernels for 3%

profile of v3, /device:TPU:97, one launch (start us, length us, event | category | flops | bytes accessed | tf_op | source)
XLA Modules:
  0.0 149.0 jit_solution(18270087267728245986)
XLA Ops:
  1.9 2.8 %collective-permute-start.1 = (f32[144,512]{1,0:T(8,128)S(1)}, f32[144,512]{1,0:T(8,128)S(1)}, u32[]{:S(2)}, u32[]{:S(2)}) collective-permute-start(f32[144,512]{1,0:T(8,128)S(1)} %constant_dynamic-update-slice_fusion.own), channel_id=1, source_target_pairs={{18,0},{3,1},{0,2},{17,3},{22,4},{7,5},{4,6},{21,7},{26,8},{11,9},... | collective-permute-start | bytes 884744 | tf_op jit(solution)/shard_map/ppermute | solution.py:463
  6.9 4.6 %invert_pair.1 = (f32[48,128]{1,0:T(8,128)}, f32[48,1]{1,0:T(8,128)}, f32[48,1]{1,0:T(8,128)S(1)}) custom-call(f32[48,128]{1,0:T(8,128)} %maximum_add_fusion.matrix_ref), custom_call_target="tpu_custom_call" | custom-call | tf_op jit(solution)/shard_map/invert_pair/pallas_call | solution.py:98
  13.7 47.6 %to_payload.1 = (f32[48,1024]{1,0:T(8,128)S(1)}, f32[48,1024]{1,0:T(8,128)S(1)}, f32[48,512]{1,0:T(8,128)}, f32[48,2048]{1,0:T(8,128)S(1)}, f32[48,2048]{1,0:T(8...) custom-call(s32[2]{0:T(128)S(1)} %pad_add_fusion.where, f32[144,512]{1,0:T(8,128)S(1)} %constant_dynamic-update-slice_fusion.own, ...), custom_call_target="tpu_custom_call" | custom-call | tf_op jit(solution)/shard_map/to_payload/pallas_call | solution.py:337
  61.3 7.7 %collective-permute-start.3 = (f32[48,1024]{1,0:T(8,128)S(1)}, f32[48,1024]{1,0:T(8,128)S(1)}, u32[]{:S(2)}, u32[]{:S(2)}) collective-permute-start(f32[48,1024]{1,0:T(8,128)S(1)} %get-tuple-element.399), channel_id=1, source_target_pairs={{20,16},{29,17},{22,18},{31,19},{16,20},{25,21},{18,22},{27,23},{2... | collective-permute-start | bytes 589832 | tf_op jit(solution)/shard_map/ppermute | solution.py:485
  69.0 1.9 %collective-permute-start.5 = (f32[48,1024]{1,0:T(8,128)S(1)}, f32[48,1024]{1,0:T(8,128)S(1)}, u32[]{:S(2)}, u32[]{:S(2)}) collective-permute-start(f32[48,1024]{1,0:T(8,128)S(1)} %get-tuple-element.399), channel_id=1, source_target_pairs={{28,16},{21,17},{30,18},{23,19},{24,20},{17,21},{26,22},{19,23},{2... | collective-permute-start | bytes 589832 | tf_op jit(solution)/shard_map/ppermute | solution.py:485
  70.9 1.1 collective-permute-done.3
  72.0 2.3 %collective-permute-start.7 = (f32[48,1024]{1,0:T(8,128)S(1)}, f32[48,1024]{1,0:T(8,128)S(1)}, u32[]{:S(2)}, u32[]{:S(2)}) collective-permute-start(f32[48,1024]{1,0:T(8,128)S(1)} %collective-permute-done.3), channel_id=1, source_target_pairs={{28,16},{21,17},{30,18},{23,19},{24,20},{17,21},{26,22},{19,23},{2... | collective-permute-start | bytes 589832 | tf_op jit(solution)/shard_map/ppermute | solution.py:485
  74.3 3.2 %collective-permute-start.4 = (f32[48,1024]{1,0:T(8,128)S(1)}, f32[48,1024]{1,0:T(8,128)S(1)}, u32[]{:S(2)}, u32[]{:S(2)}) collective-permute-start(f32[48,1024]{1,0:T(8,128)S(1)} %collective-permute-done.3), channel_id=1, source_target_pairs={{0,1},{1,0},{2,3},{3,2},{4,5},{5,4},{6,7},{7,6},{8,9},{9,8},{10,11... | collective-permute-start | bytes 589832 | tf_op jit(solution)/shard_map/ppermute | solution.py:481
  77.6 1.1 collective-permute-done.7
  78.7 2.3 %collective-permute-start.8 = (f32[48,1024]{1,0:T(8,128)S(1)}, f32[48,1024]{1,0:T(8,128)S(1)}, u32[]{:S(2)}, u32[]{:S(2)}) collective-permute-start(f32[48,1024]{1,0:T(8,128)S(1)} %collective-permute-done.7), channel_id=1, source_target_pairs={{0,1},{1,0},{2,3},{3,2},{4,5},{5,4},{6,7},{7,6},{8,9},{9,8},{10,11... | collective-permute-start | bytes 589832 | tf_op jit(solution)/shard_map/ppermute | solution.py:481
  83.3 8.9 %collective-permute-start.17 = (f32[48,1024]{1,0:T(8,128)S(1)}, f32[48,1024]{1,0:T(8,128)S(1)}, u32[]{:S(2)}, u32[]{:S(2)}) collective-permute-start(f32[48,1024]{1,0:T(8,128)S(1)} %get-tuple-element.399), channel_id=1, source_target_pairs={{80,64},{84,68},{88,72},{92,76},{64,80},{68,84},{72,88},{76,92},{1... | collective-permute-start | bytes 589832 | tf_op jit(solution)/shard_map/ppermute | solution.py:504
  92.3 1.4 collective-permute-start.11
  93.7 3.7 %collective-permute-done.17 = f32[48,1024]{1,0:T(8,128)S(1)} collective-permute-done((f32[48,1024]{1,0:T(8,128)S(1)}, f32[48,1024]{1,0:T(8,128)S(1)}, u32[]{:S(2)}, u32[]{:S(2)}) %collective-permute-start.17) | collective-permute-done | bytes 196640 | tf_op jit(solution)/shard_map/ppermute | solution.py:504
  97.4 4.8 %collective-permute-start.19 = (f32[48,1024]{1,0:T(8,128)S(1)}, f32[48,1024]{1,0:T(8,128)S(1)}, u32[]{:S(2)}, u32[]{:S(2)}) collective-permute-start(f32[48,1024]{1,0:T(8,128)S(1)} %collective-permute-done.17), channel_id=1, source_target_pairs={{68,64},{77,65},{70,66},{79,67},{64,68},{73,69},{66,70},{75,71},{7... | collective-permute-start | bytes 589832 | tf_op jit(solution)/shard_map/ppermute | solution.py:485
  102.4 1.9 %collective-permute-start.21 = (f32[48,1024]{1,0:T(8,128)S(1)}, f32[48,1024]{1,0:T(8,128)S(1)}, u32[]{:S(2)}, u32[]{:S(2)}) collective-permute-start(f32[48,1024]{1,0:T(8,128)S(1)} %collective-permute-done.17), channel_id=1, source_target_pairs={{76,64},{69,65},{78,66},{71,67},{72,68},{65,69},{74,70},{67,71},{6... | collective-permute-start | bytes 589832 | tf_op jit(solution)/shard_map/ppermute | solution.py:485
  105.4 3.0 %collective-permute-start.23 = (f32[48,1024]{1,0:T(8,128)S(1)}, f32[48,1024]{1,0:T(8,128)S(1)}, u32[]{:S(2)}, u32[]{:S(2)}) collective-permute-start(f32[48,1024]{1,0:T(8,128)S(1)} %collective-permute-done.19), channel_id=1, source_target_pairs={{76,64},{69,65},{78,66},{71,67},{72,68},{65,69},{74,70},{67,71},{6... | collective-permute-start | bytes 589832 | tf_op jit(solution)/shard_map/ppermute | solution.py:485
  108.4 1.4 collective-permute-start.15
  109.8 1.3 collective-permute-start.13
  111.1 2.6 %collective-permute-start.20 = (f32[48,1024]{1,0:T(8,128)S(1)}, f32[48,1024]{1,0:T(8,128)}, u32[]{:S(2)}, u32[]{:S(2)}) collective-permute-start(f32[48,1024]{1,0:T(8,128)S(1)} %collective-permute-done.19), channel_id=1, source_target_pairs={{0,1},{1,0},{2,3},{3,2},{4,5},{5,4},{6,7},{7,6},{8,9},{9,8},{10,11... | collective-permute-start | bytes 589832 | tf_op jit(solution)/shard_map/ppermute | solution.py:481
  116.7 1.3 collective-permute-start.25
  118.0 16.7 %collective-permute-done.25 = f32[48,1024]{1,0:T(8,128)} collective-permute-done((f32[48,1024]{1,0:T(8,128)}, f32[48,1024]{1,0:T(8,128)}, u32[]{:S(2)}, u32[]{:S(2)}) %collective-permute-start.25) | collective-permute-done | bytes 196640 | tf_op jit(solution)/shard_map/ppermute | solution.py:500
  135.6 1.4 collective-permute-done.26
  137.0 11.8 %conditional.9 = (f32[1,48,512]{2,1,0:T(8,128)}) conditional(s32[]{:T(128)} %convert_element_type.35, f32[48,512]{1,0:T(8,128)} %get-tuple-element.400, (s32[2]{0:T(128)S(1)}, s32[1]{0:T(128)}, f32[48,1024]{1,0:T(8,128)}, f32[48,1024]{1,0:T(8,128)}, f32[48,1024]{1,0:T(8,128)S(1)}, /*index=5*/f32[48,1024]{1,0:T(8,128)S(1)}, ...), branch_computations={%region_9.10_spmd, %region_10.11_spmd} | conditional | bytes 776 | solution.py:497
  137.2 11.6 %links_8_1.1 = (f32[48,1024]{1,0:T(8,128)}, f32[48,512]{1,0:T(8,128)}) custom-call(s32[2]{0:T(128)S(1)} %get-tuple-element.338.refs_0_, s32[1]{0:T(128)} %get-tuple-element.339.refs_1_, f32[48,1024]{1,0:T(8,128)} %get-tuple-element.340.refs_2_, f32[48,1024]{1,0:T(8,128)} %get-tuple-element.341.refs_3_, f32[48,1024]{1,0:T(8,128)S(1)} %get-tuple-element.342.refs_4_, ...), custom_call_target="tpu_custom_call" | custom-call | tf_op jit(solution)/shard_map/cond/branch_1_fun/links_8_1/pallas_call | solution.py:430
  (69 shorter events, 13.8 us)
Async XLA Ops:
  1.9 9.7 %collective-permute-start.1 = (f32[144,512]{1,0:T(8,128)S(1)}, f32[144,512]{1,0:T(8,128)S(1)}, u32[]{:S(2)}, u32[]{:S(2)}) collective-permute-start(f32[144,512]{1,0:T(8,128)S(1)} %constant_dynamic-update-slice_fusion.own), channel_id=1, source_target_pairs={{18,0},{3,1},{0,2},{17,3},{22,4},{7,5},{4,6},{21,7},{26,8},{11,9},... | collective-permute-start | bytes 884744 | tf_op jit(solution)/shard_map/ppermute | solution.py:463
  4.7 8.4 %collective-permute-start = (f32[144,512]{1,0:T(8,128)S(1)}, f32[144,512]{1,0:T(8,128)S(1)}, u32[]{:S(2)}, u32[]{:S(2)}) collective-permute-start(f32[144,512]{1,0:T(8,128)S(1)} %constant_dynamic-update-slice_fusion.own), channel_id=1, source_target_pairs={{0,1},{1,0},{2,3},{3,2},{4,5},{5,4},{6,7},{7,6},{8,9},{9,8},{10,11... | collective-permute-start | bytes 884744 | tf_op jit(solution)/shard_map/ppermute | solution.py:464
  61.3 10.7 %collective-permute-start.3 = (f32[48,1024]{1,0:T(8,128)S(1)}, f32[48,1024]{1,0:T(8,128)S(1)}, u32[]{:S(2)}, u32[]{:S(2)}) collective-permute-start(f32[48,1024]{1,0:T(8,128)S(1)} %get-tuple-element.399), channel_id=1, source_target_pairs={{20,16},{29,17},{22,18},{31,19},{16,20},{25,21},{18,22},{27,23},{2... | collective-permute-start | bytes 589832 | tf_op jit(solution)/shard_map/ppermute | solution.py:485
  69.0 8.5 %collective-permute-start.5 = (f32[48,1024]{1,0:T(8,128)S(1)}, f32[48,1024]{1,0:T(8,128)S(1)}, u32[]{:S(2)}, u32[]{:S(2)}) collective-permute-start(f32[48,1024]{1,0:T(8,128)S(1)} %get-tuple-element.399), channel_id=1, source_target_pairs={{28,16},{21,17},{30,18},{23,19},{24,20},{17,21},{26,22},{19,23},{2... | collective-permute-start | bytes 589832 | tf_op jit(solution)/shard_map/ppermute | solution.py:485
  72.0 6.7 %collective-permute-start.7 = (f32[48,1024]{1,0:T(8,128)S(1)}, f32[48,1024]{1,0:T(8,128)S(1)}, u32[]{:S(2)}, u32[]{:S(2)}) collective-permute-start(f32[48,1024]{1,0:T(8,128)S(1)} %collective-permute-done.3), channel_id=1, source_target_pairs={{28,16},{21,17},{30,18},{23,19},{24,20},{17,21},{26,22},{19,23},{2... | collective-permute-start | bytes 589832 | tf_op jit(solution)/shard_map/ppermute | solution.py:485
  74.3 6.8 %collective-permute-start.4 = (f32[48,1024]{1,0:T(8,128)S(1)}, f32[48,1024]{1,0:T(8,128)S(1)}, u32[]{:S(2)}, u32[]{:S(2)}) collective-permute-start(f32[48,1024]{1,0:T(8,128)S(1)} %collective-permute-done.3), channel_id=1, source_target_pairs={{0,1},{1,0},{2,3},{3,2},{4,5},{5,4},{6,7},{7,6},{8,9},{9,8},{10,11... | collective-permute-start | bytes 589832 | tf_op jit(solution)/shard_map/ppermute | solution.py:481
  77.5 3.6 %collective-permute-start.6 = (f32[48,1024]{1,0:T(8,128)S(1)}, f32[48,1024]{1,0:T(8,128)S(1)}, u32[]{:S(2)}, u32[]{:S(2)}) collective-permute-start(f32[48,1024]{1,0:T(8,128)S(1)} %collective-permute-done.5), channel_id=1, source_target_pairs={{0,1},{1,0},{2,3},{3,2},{4,5},{5,4},{6,7},{7,6},{8,9},{9,8},{10,11... | collective-permute-start | bytes 589832 | tf_op jit(solution)/shard_map/ppermute | solution.py:481
  78.7 3.4 %collective-permute-start.8 = (f32[48,1024]{1,0:T(8,128)S(1)}, f32[48,1024]{1,0:T(8,128)S(1)}, u32[]{:S(2)}, u32[]{:S(2)}) collective-permute-start(f32[48,1024]{1,0:T(8,128)S(1)} %collective-permute-done.7), channel_id=1, source_target_pairs={{0,1},{1,0},{2,3},{3,2},{4,5},{5,4},{6,7},{7,6},{8,9},{9,8},{10,11... | collective-permute-start | bytes 589832 | tf_op jit(solution)/shard_map/ppermute | solution.py:481
  82.9 9.4 %collective-permute-start.10 = (f32[48,1024]{1,0:T(8,128)S(1)}, f32[48,1024]{1,0:T(8,128)S(1)}, u32[]{:S(2)}, u32[]{:S(2)}) collective-permute-start(f32[48,1024]{1,0:T(8,128)S(1)} %collective-permute-done.9), channel_id=1, source_target_pairs={{0,1},{1,0},{2,3},{3,2},{4,5},{5,4},{6,7},{7,6},{8,9},{9,8},{10,11... | collective-permute-start | bytes 589832 | tf_op jit(solution)/shard_map/ppermute | solution.py:481
  83.3 14.1 %collective-permute-start.17 = (f32[48,1024]{1,0:T(8,128)S(1)}, f32[48,1024]{1,0:T(8,128)S(1)}, u32[]{:S(2)}, u32[]{:S(2)}) collective-permute-start(f32[48,1024]{1,0:T(8,128)S(1)} %get-tuple-element.399), channel_id=1, source_target_pairs={{80,64},{84,68},{88,72},{92,76},{64,80},{68,84},{72,88},{76,92},{1... | collective-permute-start | bytes 589832 | tf_op jit(solution)/shard_map/ppermute | solution.py:504
  92.3 9.9 %collective-permute-start.11 = (f32[48,1024]{1,0:T(8,128)S(1)}, f32[48,1024]{1,0:T(8,128)}, u32[]{:S(2)}, u32[]{:S(2)}) collective-permute-start(f32[48,1024]{1,0:T(8,128)S(1)} %get-tuple-element.397), channel_id=1, source_target_pairs={{32,48},{36,52},{40,56},{44,60},{33,49},{37,53},{41,57},{45,61},{3... | collective-permute-start | bytes 589832 | tf_op jit(solution)/shard_map/ppermute | solution.py:500
  97.4 8.0 %collective-permute-start.19 = (f32[48,1024]{1,0:T(8,128)S(1)}, f32[48,1024]{1,0:T(8,128)S(1)}, u32[]{:S(2)}, u32[]{:S(2)}) collective-permute-start(f32[48,1024]{1,0:T(8,128)S(1)} %collective-permute-done.17), channel_id=1, source_target_pairs={{68,64},{77,65},{70,66},{79,67},{64,68},{73,69},{66,70},{75,71},{7... | collective-permute-start | bytes 589832 | tf_op jit(solution)/shard_map/ppermute | solution.py:485
  102.2 6.2 %collective-permute-start.12 = (f32[48,1024]{1,0:T(8,128)}, f32[48,1024]{1,0:T(8,128)}, u32[]{:S(2)}, u32[]{:S(2)}) collective-permute-start(f32[48,1024]{1,0:T(8,128)} %collective-permute-done.11), channel_id=1, source_target_pairs={{0,1},{1,0},{2,3},{3,2},{4,5},{5,4},{6,7},{7,6},{8,9},{9,8},{10,11... | collective-permute-start | bytes 589832 | tf_op jit(solution)/shard_map/ppermute | solution.py:481
  102.4 8.8 %collective-permute-start.21 = (f32[48,1024]{1,0:T(8,128)S(1)}, f32[48,1024]{1,0:T(8,128)S(1)}, u32[]{:S(2)}, u32[]{:S(2)}) collective-permute-start(f32[48,1024]{1,0:T(8,128)S(1)} %collective-permute-done.17), channel_id=1, source_target_pairs={{76,64},{69,65},{78,66},{71,67},{72,68},{65,69},{74,70},{67,71},{6... | collective-permute-start | bytes 589832 | tf_op jit(solution)/shard_map/ppermute | solution.py:485
  104.3 9.4 %collective-permute-start.18 = (f32[48,1024]{1,0:T(8,128)S(1)}, f32[48,1024]{1,0:T(8,128)S(1)}, u32[]{:S(2)}, u32[]{:S(2)}) collective-permute-start(f32[48,1024]{1,0:T(8,128)S(1)} %collective-permute-done.17), channel_id=1, source_target_pairs={{0,1},{1,0},{2,3},{3,2},{4,5},{5,4},{6,7},{7,6},{8,9},{9,8},{10,11... | collective-permute-start | bytes 589832 | tf_op jit(solution)/shard_map/ppermute | solution.py:481
  105.4 8.4 %collective-permute-start.23 = (f32[48,1024]{1,0:T(8,128)S(1)}, f32[48,1024]{1,0:T(8,128)S(1)}, u32[]{:S(2)}, u32[]{:S(2)}) collective-permute-start(f32[48,1024]{1,0:T(8,128)S(1)} %collective-permute-done.19), channel_id=1, source_target_pairs={{76,64},{69,65},{78,66},{71,67},{72,68},{65,69},{74,70},{67,71},{6... | collective-permute-start | bytes 589832 | tf_op jit(solution)/shard_map/ppermute | solution.py:485
  108.4 6.2 %collective-permute-start.15 = (f32[48,1024]{1,0:T(8,128)}, f32[48,1024]{1,0:T(8,128)}, u32[]{:S(2)}, u32[]{:S(2)}) collective-permute-start(f32[48,1024]{1,0:T(8,128)} %get-tuple-element.398), channel_id=1, source_target_pairs={{48,80},{52,84},{56,88},{60,92},{49,81},{53,85},{57,89},{61,93},{5... | collective-permute-start | bytes 589832 | tf_op jit(solution)/shard_map/ppermute | solution.py:500
  109.8 4.9 %collective-permute-start.13 = (f32[48,1024]{1,0:T(8,128)}, f32[48,1024]{1,0:T(8,128)}, u32[]{:S(2)}, u32[]{:S(2)}) collective-permute-start(f32[48,1024]{1,0:T(8,128)} %get-tuple-element.398), channel_id=1, source_target_pairs={{48,64},{52,68},{56,72},{60,76},{49,65},{53,69},{57,73},{61,77},{5... | collective-permute-start | bytes 589832 | tf_op jit(solution)/shard_map/ppermute | solution.py:500
  111.1 4.2 %collective-permute-start.20 = (f32[48,1024]{1,0:T(8,128)S(1)}, f32[48,1024]{1,0:T(8,128)}, u32[]{:S(2)}, u32[]{:S(2)}) collective-permute-start(f32[48,1024]{1,0:T(8,128)S(1)} %collective-permute-done.19), channel_id=1, source_target_pairs={{0,1},{1,0},{2,3},{3,2},{4,5},{5,4},{6,7},{7,6},{8,9},{9,8},{10,11... | collective-permute-start | bytes 589832 | tf_op jit(solution)/shard_map/ppermute | solution.py:481
  113.8 2.2 %collective-permute-start.24 = (f32[48,1024]{1,0:T(8,128)S(1)}, f32[48,1024]{1,0:T(8,128)}, u32[]{:S(2)}, u32[]{:S(2)}) collective-permute-start(f32[48,1024]{1,0:T(8,128)S(1)} %collective-permute-done.23), channel_id=1, source_target_pairs={{0,1},{1,0},{2,3},{3,2},{4,5},{5,4},{6,7},{7,6},{8,9},{9,8},{10,11... | collective-permute-start | bytes 589832 | tf_op jit(solution)/shard_map/ppermute | solution.py:481
  114.6 1.8 %collective-permute-start.16 = (f32[48,1024]{1,0:T(8,128)}, f32[48,1024]{1,0:T(8,128)}, u32[]{:S(2)}, u32[]{:S(2)}) collective-permute-start(f32[48,1024]{1,0:T(8,128)} %collective-permute-done.15), channel_id=1, source_target_pairs={{0,1},{1,0},{2,3},{3,2},{4,5},{5,4},{6,7},{7,6},{8,9},{9,8},{10,11... | collective-permute-start | bytes 589832 | tf_op jit(solution)/shard_map/ppermute | solution.py:481
  114.6 2.1 %collective-permute-start.14 = (f32[48,1024]{1,0:T(8,128)}, f32[48,1024]{1,0:T(8,128)}, u32[]{:S(2)}, u32[]{:S(2)}) collective-permute-start(f32[48,1024]{1,0:T(8,128)} %collective-permute-done.13), channel_id=1, source_target_pairs={{0,1},{1,0},{2,3},{3,2},{4,5},{5,4},{6,7},{7,6},{8,9},{9,8},{10,11... | collective-permute-start | bytes 589832 | tf_op jit(solution)/shard_map/ppermute | solution.py:481
  116.7 18.0 %collective-permute-start.25 = (f32[48,1024]{1,0:T(8,128)}, f32[48,1024]{1,0:T(8,128)}, u32[]{:S(2)}, u32[]{:S(2)}) collective-permute-start(f32[48,1024]{1,0:T(8,128)} %get-tuple-element.401), channel_id=1, source_target_pairs={{64,96},{68,100},{72,104},{76,108},{80,112},{84,116},{88,120},{92,... | collective-permute-start | bytes 589832 | tf_op jit(solution)/shard_map/ppermute | solution.py:500
  134.7 2.3 %collective-permute-start.26 = (f32[48,1024]{1,0:T(8,128)}, f32[48,1024]{1,0:T(8,128)}, u32[]{:S(2)}, u32[]{:S(2)}) collective-permute-start(f32[48,1024]{1,0:T(8,128)} %collective-permute-done.25), channel_id=1, source_target_pairs={{0,1},{1,0},{2,3},{3,2},{4,5},{5,4},{6,7},{7,6},{8,9},{9,8},{10,11... | collective-permute-start | bytes 589832 | tf_op jit(solution)/shard_map/ppermute | solution.py:481
  (10 other events, 20.8 us)

commit v4 on v3

--- a/solution.py
+++ b/solution.py
@@ -15,7 +15,7 @@
 S = 48
 TILE = 256
 CENTRE = 0.4
-ENOUGH = 2.5e-4
+ENOUGH = 2.2e-3
 
 VMEM = pl.BlockSpec(memory_space=pltpu.VMEM)
 ANY = pl.BlockSpec(memory_space=pl.ANY)
@@ -240,7 +240,7 @@
             total[:, place(k)] = 1.0 / jnp.sum(losses, axis=0, keepdims=True)
     grid = Grid(delta, source, spread, saturation, base, change)
     fine_solver = Solver(fine, fine_mode, fine_balance, 1.0, 2, False)
-    coarse_solver = Solver(coarse, coarse_mode, balance, 1.0 / FACTOR, 3, True)
+    coarse_solver = Solver(coarse, coarse_mode, balance, 1.0 / FACTOR, 2, True)
 
     def keep_own(condition):
         @pl.when(condition)
@@ -394,7 +394,7 @@
     for copy in copies + ([] if seeded else [coming(0), coming(1)]):
         copy.wait()
     grid = Grid(delta, source, spread, saturation, base, change)
-    solver = Solver(coarse, mode, balance, 1.0 / FACTOR, 3, True)
+    solver = Solver(coarse, mode, balance, 1.0 / FACTOR, 2, True)
 
     def show(slot, state):
         @pl.when(member == slot)

time: 150 us -> 138 us (0.920)
  Pallas kernels: 63.9 us -> 54.5 us
  starting transfers between devices: 52.1 us -> 49.8 us
    pallas_call x1, Pallas kernels: 47.6 us -> 40.7 us  [run_main(): pl.pallas_call(main_kernel, out_shape=[half_grid(), half_grid(), jax.Shap...]
    pallas_call x1, Pallas kernels: 11.6 us -> 9.19 us  [run_chain(): pl.pallas_call(functools.partial(chain_kernel, length, sources), out_shap...]
  transfers between devices with their start and end apart: 27 -> 27, of which waited for: 11 -> 11; matrix products, arithmetic and copies ran while one was open for 1% -> 2% of each run, Pallas kernels for 3% -> 3%
where the time goes in v4:
time: 138 us
  Pallas kernels  54.5 us (39%)
  starting transfers between devices  49.8 us (36%)
  waiting for transfers between devices  27.1 us (20%)
  local copies, waits for them, and re-layouts  3.85 us (3%)
  other arithmetic  1.88 us (1%)
    pallas_call x1, Pallas kernels, run_main(): pl.pallas_call(main_kernel, out_shape=[half_grid(), half_grid(), jax.Shap...  40.7 us
    ppermute x6, starting transfers between devices, exchanged(): return lax.ppermute(piece, ('tm', 'space'), route)  20.7 us
    ppermute x5, waiting for transfers between devices, hop(): lax.ppermute(last, 'tm', [(start - distance + m, start + m) for m in rang...  16.9 us
    ppermute x12, starting transfers between devices, swapped(): return [piece, lax.ppermute(piece, 'space', swap)]  12.1 us
    pallas_call x1, Pallas kernels, run_chain(): pl.pallas_call(functools.partial(chain_kernel, length, sources), out_shap...  9.19 us
    ppermute x1, starting transfers between devices, per_device(): lax.ppermute(behind, 'tm', [(i ^ 4, i) for i in range(16, 32)])  7.68 us
    ppermute x5, starting transfers between devices, hop(): lax.ppermute(last, 'tm', [(start - distance + m, start + m) for m in rang...  6.02 us
    pallas_call x1, Pallas kernels, invert_pair(): pl.pallas_call(invert_kernel, out_shape=[jax.ShapeDtypeStruct((S, COLS),...  4.57 us
  transfers between devices with their start and end apart: 27, of which 11 were waited for; matrix products, arithmetic and copies ran while one was open for 2% of the time, Pallas kernels for 3%

profile of v4, /device:TPU:97, one launch (start us, length us, event | category | flops | bytes accessed | tf_op | source)
XLA Modules:
  0.0 137.5 jit_solution(12734843955848377427)
XLA Ops:
  1.9 2.8 %collective-permute-start.1 = (f32[144,512]{1,0:T(8,128)S(1)}, f32[144,512]{1,0:T(8,128)S(1)}, u32[]{:S(2)}, u32[]{:S(2)}) collective-permute-start(f32[144,512]{1,0:T(8,128)S(1)} %constant_dynamic-update-slice_fusion.own), channel_id=1, source_target_pairs={{18,0},{3,1},{0,2},{17,3},{22,4},{7,5},{4,6},{21,7},{26,8},{11,9},... | collective-permute-start | bytes 884744 | tf_op jit(solution)/shard_map/ppermute | solution.py:463
  6.9 4.6 %invert_pair.1 = (f32[48,128]{1,0:T(8,128)}, f32[48,1]{1,0:T(8,128)}, f32[48,1]{1,0:T(8,128)S(1)}) custom-call(f32[48,128]{1,0:T(8,128)} %maximum_add_fusion.matrix_ref), custom_call_target="tpu_custom_call" | custom-call | tf_op jit(solution)/shard_map/invert_pair/pallas_call | solution.py:98
  13.7 40.7 %to_payload.1 = (f32[48,1024]{1,0:T(8,128)S(1)}, f32[48,1024]{1,0:T(8,128)S(1)}, f32[48,512]{1,0:T(8,128)}, f32[48,2048]{1,0:T(8,128)S(1)}, f32[48,2048]{1,0:T(8...) custom-call(s32[2]{0:T(128)S(1)} %pad_add_fusion.where, f32[144,512]{1,0:T(8,128)S(1)} %constant_dynamic-update-slice_fusion.own, ...), custom_call_target="tpu_custom_call" | custom-call | tf_op jit(solution)/shard_map/to_payload/pallas_call | solution.py:337
  54.4 6.7 %collective-permute-start.3 = (f32[48,1024]{1,0:T(8,128)S(1)}, f32[48,1024]{1,0:T(8,128)S(1)}, u32[]{:S(2)}, u32[]{:S(2)}) collective-permute-start(f32[48,1024]{1,0:T(8,128)S(1)} %get-tuple-element.399), channel_id=1, source_target_pairs={{20,16},{29,17},{22,18},{31,19},{16,20},{25,21},{18,22},{27,23},{2... | collective-permute-start | bytes 589832 | tf_op jit(solution)/shard_map/ppermute | solution.py:485
  61.1 1.9 %collective-permute-start.5 = (f32[48,1024]{1,0:T(8,128)S(1)}, f32[48,1024]{1,0:T(8,128)S(1)}, u32[]{:S(2)}, u32[]{:S(2)}) collective-permute-start(f32[48,1024]{1,0:T(8,128)S(1)} %get-tuple-element.399), channel_id=1, source_target_pairs={{28,16},{21,17},{30,18},{23,19},{24,20},{17,21},{26,22},{19,23},{2... | collective-permute-start | bytes 589832 | tf_op jit(solution)/shard_map/ppermute | solution.py:485
  63.1 1.1 collective-permute-done.3
  64.2 2.3 %collective-permute-start.7 = (f32[48,1024]{1,0:T(8,128)S(1)}, f32[48,1024]{1,0:T(8,128)S(1)}, u32[]{:S(2)}, u32[]{:S(2)}) collective-permute-start(f32[48,1024]{1,0:T(8,128)S(1)} %collective-permute-done.3), channel_id=1, source_target_pairs={{28,16},{21,17},{30,18},{23,19},{24,20},{17,21},{26,22},{19,23},{2... | collective-permute-start | bytes 589832 | tf_op jit(solution)/shard_map/ppermute | solution.py:485
  66.4 3.2 %collective-permute-start.4 = (f32[48,1024]{1,0:T(8,128)S(1)}, f32[48,1024]{1,0:T(8,128)S(1)}, u32[]{:S(2)}, u32[]{:S(2)}) collective-permute-start(f32[48,1024]{1,0:T(8,128)S(1)} %collective-permute-done.3), channel_id=1, source_target_pairs={{0,1},{1,0},{2,3},{3,2},{4,5},{5,4},{6,7},{7,6},{8,9},{9,8},{10,11... | collective-permute-start | bytes 589832 | tf_op jit(solution)/shard_map/ppermute | solution.py:481
  69.7 1.1 collective-permute-done.7
  70.9 2.3 %collective-permute-start.8 = (f32[48,1024]{1,0:T(8,128)S(1)}, f32[48,1024]{1,0:T(8,128)S(1)}, u32[]{:S(2)}, u32[]{:S(2)}) collective-permute-start(f32[48,1024]{1,0:T(8,128)S(1)} %collective-permute-done.7), channel_id=1, source_target_pairs={{0,1},{1,0},{2,3},{3,2},{4,5},{5,4},{6,7},{7,6},{8,9},{9,8},{10,11... | collective-permute-start | bytes 589832 | tf_op jit(solution)/shard_map/ppermute | solution.py:481
  75.4 7.7 %collective-permute-start.17 = (f32[48,1024]{1,0:T(8,128)S(1)}, f32[48,1024]{1,0:T(8,128)S(1)}, u32[]{:S(2)}, u32[]{:S(2)}) collective-permute-start(f32[48,1024]{1,0:T(8,128)S(1)} %get-tuple-element.399), channel_id=1, source_target_pairs={{80,64},{84,68},{88,72},{92,76},{64,80},{68,84},{72,88},{76,92},{1... | collective-permute-start | bytes 589832 | tf_op jit(solution)/shard_map/ppermute | solution.py:504
  83.1 1.4 collective-permute-start.11
  84.5 3.7 %collective-permute-done.17 = f32[48,1024]{1,0:T(8,128)S(1)} collective-permute-done((f32[48,1024]{1,0:T(8,128)S(1)}, f32[48,1024]{1,0:T(8,128)S(1)}, u32[]{:S(2)}, u32[]{:S(2)}) %collective-permute-start.17) | collective-permute-done | bytes 196640 | tf_op jit(solution)/shard_map/ppermute | solution.py:504
  88.2 4.8 %collective-permute-start.19 = (f32[48,1024]{1,0:T(8,128)S(1)}, f32[48,1024]{1,0:T(8,128)S(1)}, u32[]{:S(2)}, u32[]{:S(2)}) collective-permute-start(f32[48,1024]{1,0:T(8,128)S(1)} %collective-permute-done.17), channel_id=1, source_target_pairs={{68,64},{77,65},{70,66},{79,67},{64,68},{73,69},{66,70},{75,71},{7... | collective-permute-start | bytes 589832 | tf_op jit(solution)/shard_map/ppermute | solution.py:485
  93.2 1.9 %collective-permute-start.21 = (f32[48,1024]{1,0:T(8,128)S(1)}, f32[48,1024]{1,0:T(8,128)S(1)}, u32[]{:S(2)}, u32[]{:S(2)}) collective-permute-start(f32[48,1024]{1,0:T(8,128)S(1)} %collective-permute-done.17), channel_id=1, source_target_pairs={{76,64},{69,65},{78,66},{71,67},{72,68},{65,69},{74,70},{67,71},{6... | collective-permute-start | bytes 589832 | tf_op jit(solution)/shard_map/ppermute | solution.py:485
  96.2 3.0 %collective-permute-start.23 = (f32[48,1024]{1,0:T(8,128)S(1)}, f32[48,1024]{1,0:T(8,128)S(1)}, u32[]{:S(2)}, u32[]{:S(2)}) collective-permute-start(f32[48,1024]{1,0:T(8,128)S(1)} %collective-permute-done.19), channel_id=1, source_target_pairs={{76,64},{69,65},{78,66},{71,67},{72,68},{65,69},{74,70},{67,71},{6... | collective-permute-start | bytes 589832 | tf_op jit(solution)/shard_map/ppermute | solution.py:485
  99.3 1.4 collective-permute-start.15
  100.6 1.3 collective-permute-start.13
  102.0 2.6 %collective-permute-start.20 = (f32[48,1024]{1,0:T(8,128)S(1)}, f32[48,1024]{1,0:T(8,128)}, u32[]{:S(2)}, u32[]{:S(2)}) collective-permute-start(f32[48,1024]{1,0:T(8,128)S(1)} %collective-permute-done.19), channel_id=1, source_target_pairs={{0,1},{1,0},{2,3},{3,2},{4,5},{5,4},{6,7},{7,6},{8,9},{9,8},{10,11... | collective-permute-start | bytes 589832 | tf_op jit(solution)/shard_map/ppermute | solution.py:481
  107.5 1.3 collective-permute-start.25
  108.8 16.8 %collective-permute-done.25 = f32[48,1024]{1,0:T(8,128)} collective-permute-done((f32[48,1024]{1,0:T(8,128)}, f32[48,1024]{1,0:T(8,128)}, u32[]{:S(2)}, u32[]{:S(2)}) %collective-permute-start.25) | collective-permute-done | bytes 196640 | tf_op jit(solution)/shard_map/ppermute | solution.py:500
  126.6 1.4 %collective-permute-done.26 = f32[48,1024]{1,0:T(8,128)} collective-permute-done((f32[48,1024]{1,0:T(8,128)}, f32[48,1024]{1,0:T(8,128)}, u32[]{:S(2)}, u32[]{:S(2)}) %collective-permute-start.26) | collective-permute-done | bytes 196640 | tf_op jit(solution)/shard_map/ppermute | solution.py:481
  128.0 9.4 %conditional.9 = (f32[1,48,512]{2,1,0:T(8,128)}) conditional(s32[]{:T(128)} %convert_element_type.35, f32[48,512]{1,0:T(8,128)} %get-tuple-element.400, (s32[2]{0:T(128)S(1)}, s32[1]{0:T(128)}, f32[48,1024]{1,0:T(8,128)}, f32[48,1024]{1,0:T(8,128)}, f32[48,1024]{1,0:T(8,128)S(1)}, /*index=5*/f32[48,1024]{1,0:T(8,128)S(1)}, ...), branch_computations={%region_9.10_spmd, %region_10.11_spmd} | conditional | bytes 776 | solution.py:497
  128.2 9.2 %links_8_1.1 = (f32[48,1024]{1,0:T(8,128)}, f32[48,512]{1,0:T(8,128)}) custom-call(s32[2]{0:T(128)S(1)} %get-tuple-element.338.refs_0_, s32[1]{0:T(128)} %get-tuple-element.339.refs_1_, f32[48,1024]{1,0:T(8,128)} %get-tuple-element.340.refs_2_, f32[48,1024]{1,0:T(8,128)} %get-tuple-element.341.refs_3_, f32[48,1024]{1,0:T(8,128)S(1)} %get-tuple-element.342.refs_4_, ...), custom_call_target="tpu_custom_call" | custom-call | tf_op jit(solution)/shard_map/cond/branch_1_fun/links_8_1/pallas_call | solution.py:430
  (69 shorter events, 13.8 us)
Async XLA Ops:
  1.9 9.7 %collective-permute-start.1 = (f32[144,512]{1,0:T(8,128)S(1)}, f32[144,512]{1,0:T(8,128)S(1)}, u32[]{:S(2)}, u32[]{:S(2)}) collective-permute-start(f32[144,512]{1,0:T(8,128)S(1)} %constant_dynamic-update-slice_fusion.own), channel_id=1, source_target_pairs={{18,0},{3,1},{0,2},{17,3},{22,4},{7,5},{4,6},{21,7},{26,8},{11,9},... | collective-permute-start | bytes 884744 | tf_op jit(solution)/shard_map/ppermute | solution.py:463
  4.7 8.4 %collective-permute-start = (f32[144,512]{1,0:T(8,128)S(1)}, f32[144,512]{1,0:T(8,128)S(1)}, u32[]{:S(2)}, u32[]{:S(2)}) collective-permute-start(f32[144,512]{1,0:T(8,128)S(1)} %constant_dynamic-update-slice_fusion.own), channel_id=1, source_target_pairs={{0,1},{1,0},{2,3},{3,2},{4,5},{5,4},{6,7},{7,6},{8,9},{9,8},{10,11... | collective-permute-start | bytes 884744 | tf_op jit(solution)/shard_map/ppermute | solution.py:464
  54.4 9.8 %collective-permute-start.3 = (f32[48,1024]{1,0:T(8,128)S(1)}, f32[48,1024]{1,0:T(8,128)S(1)}, u32[]{:S(2)}, u32[]{:S(2)}) collective-permute-start(f32[48,1024]{1,0:T(8,128)S(1)} %get-tuple-element.399), channel_id=1, source_target_pairs={{20,16},{29,17},{22,18},{31,19},{16,20},{25,21},{18,22},{27,23},{2... | collective-permute-start | bytes 589832 | tf_op jit(solution)/shard_map/ppermute | solution.py:485
  61.1 8.5 %collective-permute-start.5 = (f32[48,1024]{1,0:T(8,128)S(1)}, f32[48,1024]{1,0:T(8,128)S(1)}, u32[]{:S(2)}, u32[]{:S(2)}) collective-permute-start(f32[48,1024]{1,0:T(8,128)S(1)} %get-tuple-element.399), channel_id=1, source_target_pairs={{28,16},{21,17},{30,18},{23,19},{24,20},{17,21},{26,22},{19,23},{2... | collective-permute-start | bytes 589832 | tf_op jit(solution)/shard_map/ppermute | solution.py:485
  64.2 6.7 %collective-permute-start.7 = (f32[48,1024]{1,0:T(8,128)S(1)}, f32[48,1024]{1,0:T(8,128)S(1)}, u32[]{:S(2)}, u32[]{:S(2)}) collective-permute-start(f32[48,1024]{1,0:T(8,128)S(1)} %collective-permute-done.3), channel_id=1, source_target_pairs={{28,16},{21,17},{30,18},{23,19},{24,20},{17,21},{26,22},{19,23},{2... | collective-permute-start | bytes 589832 | tf_op jit(solution)/shard_map/ppermute | solution.py:485
  66.4 6.8 %collective-permute-start.4 = (f32[48,1024]{1,0:T(8,128)S(1)}, f32[48,1024]{1,0:T(8,128)S(1)}, u32[]{:S(2)}, u32[]{:S(2)}) collective-permute-start(f32[48,1024]{1,0:T(8,128)S(1)} %collective-permute-done.3), channel_id=1, source_target_pairs={{0,1},{1,0},{2,3},{3,2},{4,5},{5,4},{6,7},{7,6},{8,9},{9,8},{10,11... | collective-permute-start | bytes 589832 | tf_op jit(solution)/shard_map/ppermute | solution.py:481
  69.6 3.6 %collective-permute-start.6 = (f32[48,1024]{1,0:T(8,128)S(1)}, f32[48,1024]{1,0:T(8,128)S(1)}, u32[]{:S(2)}, u32[]{:S(2)}) collective-permute-start(f32[48,1024]{1,0:T(8,128)S(1)} %collective-permute-done.5), channel_id=1, source_target_pairs={{0,1},{1,0},{2,3},{3,2},{4,5},{5,4},{6,7},{7,6},{8,9},{9,8},{10,11... | collective-permute-start | bytes 589832 | tf_op jit(solution)/shard_map/ppermute | solution.py:481
  70.9 3.4 %collective-permute-start.8 = (f32[48,1024]{1,0:T(8,128)S(1)}, f32[48,1024]{1,0:T(8,128)S(1)}, u32[]{:S(2)}, u32[]{:S(2)}) collective-permute-start(f32[48,1024]{1,0:T(8,128)S(1)} %collective-permute-done.7), channel_id=1, source_target_pairs={{0,1},{1,0},{2,3},{3,2},{4,5},{5,4},{6,7},{7,6},{8,9},{9,8},{10,11... | collective-permute-start | bytes 589832 | tf_op jit(solution)/shard_map/ppermute | solution.py:481
  75.0 8.1 %collective-permute-start.10 = (f32[48,1024]{1,0:T(8,128)S(1)}, f32[48,1024]{1,0:T(8,128)S(1)}, u32[]{:S(2)}, u32[]{:S(2)}) collective-permute-start(f32[48,1024]{1,0:T(8,128)S(1)} %collective-permute-done.9), channel_id=1, source_target_pairs={{0,1},{1,0},{2,3},{3,2},{4,5},{5,4},{6,7},{7,6},{8,9},{9,8},{10,11... | collective-permute-start | bytes 589832 | tf_op jit(solution)/shard_map/ppermute | solution.py:481
  75.4 12.8 %collective-permute-start.17 = (f32[48,1024]{1,0:T(8,128)S(1)}, f32[48,1024]{1,0:T(8,128)S(1)}, u32[]{:S(2)}, u32[]{:S(2)}) collective-permute-start(f32[48,1024]{1,0:T(8,128)S(1)} %get-tuple-element.399), channel_id=1, source_target_pairs={{80,64},{84,68},{88,72},{92,76},{64,80},{68,84},{72,88},{76,92},{1... | collective-permute-start | bytes 589832 | tf_op jit(solution)/shard_map/ppermute | solution.py:504
  83.1 9.9 %collective-permute-start.11 = (f32[48,1024]{1,0:T(8,128)S(1)}, f32[48,1024]{1,0:T(8,128)}, u32[]{:S(2)}, u32[]{:S(2)}) collective-permute-start(f32[48,1024]{1,0:T(8,128)S(1)} %get-tuple-element.397), channel_id=1, source_target_pairs={{32,48},{36,52},{40,56},{44,60},{33,49},{37,53},{41,57},{45,61},{3... | collective-permute-start | bytes 589832 | tf_op jit(solution)/shard_map/ppermute | solution.py:500
  88.2 8.0 %collective-permute-start.19 = (f32[48,1024]{1,0:T(8,128)S(1)}, f32[48,1024]{1,0:T(8,128)S(1)}, u32[]{:S(2)}, u32[]{:S(2)}) collective-permute-start(f32[48,1024]{1,0:T(8,128)S(1)} %collective-permute-done.17), channel_id=1, source_target_pairs={{68,64},{77,65},{70,66},{79,67},{64,68},{73,69},{66,70},{75,71},{7... | collective-permute-start | bytes 589832 | tf_op jit(solution)/shard_map/ppermute | solution.py:485
  93.1 6.2 %collective-permute-start.12 = (f32[48,1024]{1,0:T(8,128)}, f32[48,1024]{1,0:T(8,128)}, u32[]{:S(2)}, u32[]{:S(2)}) collective-permute-start(f32[48,1024]{1,0:T(8,128)} %collective-permute-done.11), channel_id=1, source_target_pairs={{0,1},{1,0},{2,3},{3,2},{4,5},{5,4},{6,7},{7,6},{8,9},{9,8},{10,11... | collective-permute-start | bytes 589832 | tf_op jit(solution)/shard_map/ppermute | solution.py:481
  93.2 8.8 %collective-permute-start.21 = (f32[48,1024]{1,0:T(8,128)S(1)}, f32[48,1024]{1,0:T(8,128)S(1)}, u32[]{:S(2)}, u32[]{:S(2)}) collective-permute-start(f32[48,1024]{1,0:T(8,128)S(1)} %collective-permute-done.17), channel_id=1, source_target_pairs={{76,64},{69,65},{78,66},{71,67},{72,68},{65,69},{74,70},{67,71},{6... | collective-permute-start | bytes 589832 | tf_op jit(solution)/shard_map/ppermute | solution.py:485
  95.1 9.4 %collective-permute-start.18 = (f32[48,1024]{1,0:T(8,128)S(1)}, f32[48,1024]{1,0:T(8,128)S(1)}, u32[]{:S(2)}, u32[]{:S(2)}) collective-permute-start(f32[48,1024]{1,0:T(8,128)S(1)} %collective-permute-done.17), channel_id=1, source_target_pairs={{0,1},{1,0},{2,3},{3,2},{4,5},{5,4},{6,7},{7,6},{8,9},{9,8},{10,11... | collective-permute-start | bytes 589832 | tf_op jit(solution)/shard_map/ppermute | solution.py:481
  96.2 8.4 %collective-permute-start.23 = (f32[48,1024]{1,0:T(8,128)S(1)}, f32[48,1024]{1,0:T(8,128)S(1)}, u32[]{:S(2)}, u32[]{:S(2)}) collective-permute-start(f32[48,1024]{1,0:T(8,128)S(1)} %collective-permute-done.19), channel_id=1, source_target_pairs={{76,64},{69,65},{78,66},{71,67},{72,68},{65,69},{74,70},{67,71},{6... | collective-permute-start | bytes 589832 | tf_op jit(solution)/shard_map/ppermute | solution.py:485
  99.3 6.2 %collective-permute-start.15 = (f32[48,1024]{1,0:T(8,128)}, f32[48,1024]{1,0:T(8,128)}, u32[]{:S(2)}, u32[]{:S(2)}) collective-permute-start(f32[48,1024]{1,0:T(8,128)} %get-tuple-element.398), channel_id=1, source_target_pairs={{48,80},{52,84},{56,88},{60,92},{49,81},{53,85},{57,89},{61,93},{5... | collective-permute-start | bytes 589832 | tf_op jit(solution)/shard_map/ppermute | solution.py:500
  100.6 4.9 %collective-permute-start.13 = (f32[48,1024]{1,0:T(8,128)}, f32[48,1024]{1,0:T(8,128)}, u32[]{:S(2)}, u32[]{:S(2)}) collective-permute-start(f32[48,1024]{1,0:T(8,128)} %get-tuple-element.398), channel_id=1, source_target_pairs={{48,64},{52,68},{56,72},{60,76},{49,65},{53,69},{57,73},{61,77},{5... | collective-permute-start | bytes 589832 | tf_op jit(solution)/shard_map/ppermute | solution.py:500
  102.0 4.2 %collective-permute-start.20 = (f32[48,1024]{1,0:T(8,128)S(1)}, f32[48,1024]{1,0:T(8,128)}, u32[]{:S(2)}, u32[]{:S(2)}) collective-permute-start(f32[48,1024]{1,0:T(8,128)S(1)} %collective-permute-done.19), channel_id=1, source_target_pairs={{0,1},{1,0},{2,3},{3,2},{4,5},{5,4},{6,7},{7,6},{8,9},{9,8},{10,11... | collective-permute-start | bytes 589832 | tf_op jit(solution)/shard_map/ppermute | solution.py:481
  104.7 2.2 %collective-permute-start.24 = (f32[48,1024]{1,0:T(8,128)S(1)}, f32[48,1024]{1,0:T(8,128)}, u32[]{:S(2)}, u32[]{:S(2)}) collective-permute-start(f32[48,1024]{1,0:T(8,128)S(1)} %collective-permute-done.23), channel_id=1, source_target_pairs={{0,1},{1,0},{2,3},{3,2},{4,5},{5,4},{6,7},{7,6},{8,9},{9,8},{10,11... | collective-permute-start | bytes 589832 | tf_op jit(solution)/shard_map/ppermute | solution.py:481
  105.5 1.8 %collective-permute-start.16 = (f32[48,1024]{1,0:T(8,128)}, f32[48,1024]{1,0:T(8,128)}, u32[]{:S(2)}, u32[]{:S(2)}) collective-permute-start(f32[48,1024]{1,0:T(8,128)} %collective-permute-done.15), channel_id=1, source_target_pairs={{0,1},{1,0},{2,3},{3,2},{4,5},{5,4},{6,7},{7,6},{8,9},{9,8},{10,11... | collective-permute-start | bytes 589832 | tf_op jit(solution)/shard_map/ppermute | solution.py:481
  105.5 2.1 %collective-permute-start.14 = (f32[48,1024]{1,0:T(8,128)}, f32[48,1024]{1,0:T(8,128)}, u32[]{:S(2)}, u32[]{:S(2)}) collective-permute-start(f32[48,1024]{1,0:T(8,128)} %collective-permute-done.13), channel_id=1, source_target_pairs={{0,1},{1,0},{2,3},{3,2},{4,5},{5,4},{6,7},{7,6},{8,9},{9,8},{10,11... | collective-permute-start | bytes 589832 | tf_op jit(solution)/shard_map/ppermute | solution.py:481
  107.5 18.1 %collective-permute-start.25 = (f32[48,1024]{1,0:T(8,128)}, f32[48,1024]{1,0:T(8,128)}, u32[]{:S(2)}, u32[]{:S(2)}) collective-permute-start(f32[48,1024]{1,0:T(8,128)} %get-tuple-element.401), channel_id=1, source_target_pairs={{64,96},{68,100},{72,104},{76,108},{80,112},{84,116},{88,120},{92,... | collective-permute-start | bytes 589832 | tf_op jit(solution)/shard_map/ppermute | solution.py:500
  125.7 2.3 %collective-permute-start.26 = (f32[48,1024]{1,0:T(8,128)}, f32[48,1024]{1,0:T(8,128)}, u32[]{:S(2)}, u32[]{:S(2)}) collective-permute-start(f32[48,1024]{1,0:T(8,128)} %collective-permute-done.25), channel_id=1, source_target_pairs={{0,1},{1,0},{2,3},{3,2},{4,5},{5,4},{6,7},{7,6},{8,9},{9,8},{10,11... | collective-permute-start | bytes 589832 | tf_op jit(solution)/shard_map/ppermute | solution.py:481
  (10 other events, 20.8 us)

commit v5 on v4

--- a/solution.py
+++ b/solution.py
@@ -405,23 +405,26 @@
         for k in range(2):
             held(payloads[k], slot, k).wait()
 
-    def link(slot, carry):
+    def link(slot, before, after):
         fetched_payload(slot)
 
         def linked(at, moved, _):
-            middle[:, at] = field[:, at] + moved + stage[slot, :, at]
-
-        grid.solve(solver, field, None, counts[0], linked)
-        for at in TILES:
-            field[:, at] = middle[:, at]
-        show(slot, field)
+            after[:, at] = before[:, at] + moved + stage[slot, :, at]
+
+        grid.solve(solver, before, None, counts[0], linked)
+        show(slot, after)
+
+    def two_links(pair, carry):
+        link(2 * pair, field, middle)
+        link(2 * pair + 1, middle, field)
         return carry
 
     if seeded:
         fetched_payload(0)
-        field[...] = stage[0]
-        show(0, field)
-    lax.fori_loop(1 if seeded else 0, length, link, 0)
+        middle[...] = stage[0]
+        show(0, middle)
+        link(1, middle, field)
+    lax.fori_loop(1 if seeded else 0, length // 2, two_links, 0)
     half[...] = field[:, half_at(strip, 0)]
 
 

time: 138 us -> 138 us (level)
  no operation moved by 1% of the time
where the time goes in v5:
time: 138 us; the launch traced here: 137 us
  Pallas kernels  54.3 us (39%)
  starting transfers between devices  49.6 us (36%)
  waiting for transfers between devices  27.1 us (20%)
  local copies, waits for them, and re-layouts  3.85 us (3%)
  other arithmetic  1.88 us (1%)
    pallas_call x1, Pallas kernels, run_main(): pl.pallas_call(main_kernel, out_shape=[half_grid(), half_grid(), jax.Shap...  40.7 us
    ppermute x6, starting transfers between devices, exchanged(): return lax.ppermute(piece, ('tm', 'space'), route)  20.7 us
    ppermute x5, waiting for transfers between devices, hop(): lax.ppermute(last, 'tm', [(start - distance + m, start + m) for m in rang...  16.8 us
    ppermute x12, starting transfers between devices, swapped(): return [piece, lax.ppermute(piece, 'space', swap)]  11.9 us
    pallas_call x1, Pallas kernels, run_chain(): pl.pallas_call(functools.partial(chain_kernel, length, sources), out_shap...  8.99 us
    ppermute x1, starting transfers between devices, per_device(): lax.ppermute(behind, 'tm', [(i ^ 4, i) for i in range(16, 32)])  7.68 us
    ppermute x5, starting transfers between devices, hop(): lax.ppermute(last, 'tm', [(start - distance + m, start + m) for m in rang...  6.02 us
    pallas_call x1, Pallas kernels, invert_pair(): pl.pallas_call(invert_kernel, out_shape=[jax.ShapeDtypeStruct((S, COLS),...  4.57 us
  transfers between devices with their start and end apart: 27, of which 11 were waited for; matrix products, arithmetic and copies ran while one was open for 2% of the time, Pallas kernels for 3%

profile of v5, /device:TPU:97, one launch (start us, length us, event | category | flops | bytes accessed | tf_op | source)
XLA Modules:
  0.0 137.3 jit_solution(18006354401873136407)
XLA Ops:
  1.9 2.8 %collective-permute-start.1 = (f32[144,512]{1,0:T(8,128)S(1)}, f32[144,512]{1,0:T(8,128)S(1)}, u32[]{:S(2)}, u32[]{:S(2)}) collective-permute-start(f32[144,512]{1,0:T(8,128)S(1)} %constant_dynamic-update-slice_fusion.own), channel_id=1, source_target_pairs={{18,0},{3,1},{0,2},{17,3},{22,4},{7,5},{4,6},{21,7},{26,8},{11,9},... | collective-permute-start | bytes 884744 | tf_op jit(solution)/shard_map/ppermute | solution.py:466
  6.9 4.6 %invert_pair.1 = (f32[48,128]{1,0:T(8,128)}, f32[48,1]{1,0:T(8,128)}, f32[48,1]{1,0:T(8,128)S(1)}) custom-call(f32[48,128]{1,0:T(8,128)} %maximum_add_fusion.matrix_ref), custom_call_target="tpu_custom_call" | custom-call | tf_op jit(solution)/shard_map/invert_pair/pallas_call | solution.py:98
  13.7 40.7 %to_payload.1 = (f32[48,1024]{1,0:T(8,128)S(1)}, f32[48,1024]{1,0:T(8,128)S(1)}, f32[48,512]{1,0:T(8,128)}, f32[48,2048]{1,0:T(8,128)S(1)}, f32[48,2048]{1,0:T(8...) custom-call(s32[2]{0:T(128)S(1)} %pad_add_fusion.where, f32[144,512]{1,0:T(8,128)S(1)} %constant_dynamic-update-slice_fusion.own, ...), custom_call_target="tpu_custom_call" | custom-call | tf_op jit(solution)/shard_map/to_payload/pallas_call | solution.py:337
  54.4 6.7 %collective-permute-start.3 = (f32[48,1024]{1,0:T(8,128)S(1)}, f32[48,1024]{1,0:T(8,128)S(1)}, u32[]{:S(2)}, u32[]{:S(2)}) collective-permute-start(f32[48,1024]{1,0:T(8,128)S(1)} %get-tuple-element.399), channel_id=1, source_target_pairs={{20,16},{29,17},{22,18},{31,19},{16,20},{25,21},{18,22},{27,23},{2... | collective-permute-start | bytes 589832 | tf_op jit(solution)/shard_map/ppermute | solution.py:488
  61.1 1.9 %collective-permute-start.5 = (f32[48,1024]{1,0:T(8,128)S(1)}, f32[48,1024]{1,0:T(8,128)S(1)}, u32[]{:S(2)}, u32[]{:S(2)}) collective-permute-start(f32[48,1024]{1,0:T(8,128)S(1)} %get-tuple-element.399), channel_id=1, source_target_pairs={{28,16},{21,17},{30,18},{23,19},{24,20},{17,21},{26,22},{19,23},{2... | collective-permute-start | bytes 589832 | tf_op jit(solution)/shard_map/ppermute | solution.py:488
  63.1 1.1 collective-permute-done.3
  64.2 2.3 %collective-permute-start.7 = (f32[48,1024]{1,0:T(8,128)S(1)}, f32[48,1024]{1,0:T(8,128)S(1)}, u32[]{:S(2)}, u32[]{:S(2)}) collective-permute-start(f32[48,1024]{1,0:T(8,128)S(1)} %collective-permute-done.3), channel_id=1, source_target_pairs={{28,16},{21,17},{30,18},{23,19},{24,20},{17,21},{26,22},{19,23},{2... | collective-permute-start | bytes 589832 | tf_op jit(solution)/shard_map/ppermute | solution.py:488
  66.4 3.2 %collective-permute-start.4 = (f32[48,1024]{1,0:T(8,128)S(1)}, f32[48,1024]{1,0:T(8,128)S(1)}, u32[]{:S(2)}, u32[]{:S(2)}) collective-permute-start(f32[48,1024]{1,0:T(8,128)S(1)} %collective-permute-done.3), channel_id=1, source_target_pairs={{0,1},{1,0},{2,3},{3,2},{4,5},{5,4},{6,7},{7,6},{8,9},{9,8},{10,11... | collective-permute-start | bytes 589832 | tf_op jit(solution)/shard_map/ppermute | solution.py:484
  69.7 1.1 collective-permute-done.7
  70.9 2.3 %collective-permute-start.8 = (f32[48,1024]{1,0:T(8,128)S(1)}, f32[48,1024]{1,0:T(8,128)S(1)}, u32[]{:S(2)}, u32[]{:S(2)}) collective-permute-start(f32[48,1024]{1,0:T(8,128)S(1)} %collective-permute-done.7), channel_id=1, source_target_pairs={{0,1},{1,0},{2,3},{3,2},{4,5},{5,4},{6,7},{7,6},{8,9},{9,8},{10,11... | collective-permute-start | bytes 589832 | tf_op jit(solution)/shard_map/ppermute | solution.py:484
  75.4 7.7 %collective-permute-start.17 = (f32[48,1024]{1,0:T(8,128)S(1)}, f32[48,1024]{1,0:T(8,128)S(1)}, u32[]{:S(2)}, u32[]{:S(2)}) collective-permute-start(f32[48,1024]{1,0:T(8,128)S(1)} %get-tuple-element.399), channel_id=1, source_target_pairs={{80,64},{84,68},{88,72},{92,76},{64,80},{68,84},{72,88},{76,92},{1... | collective-permute-start | bytes 589832 | tf_op jit(solution)/shard_map/ppermute | solution.py:507
  83.1 1.4 collective-permute-start.11
  84.5 3.7 %collective-permute-done.17 = f32[48,1024]{1,0:T(8,128)S(1)} collective-permute-done((f32[48,1024]{1,0:T(8,128)S(1)}, f32[48,1024]{1,0:T(8,128)S(1)}, u32[]{:S(2)}, u32[]{:S(2)}) %collective-permute-start.17) | collective-permute-done | bytes 196640 | tf_op jit(solution)/shard_map/ppermute | solution.py:507
  88.2 4.8 %collective-permute-start.19 = (f32[48,1024]{1,0:T(8,128)S(1)}, f32[48,1024]{1,0:T(8,128)S(1)}, u32[]{:S(2)}, u32[]{:S(2)}) collective-permute-start(f32[48,1024]{1,0:T(8,128)S(1)} %collective-permute-done.17), channel_id=1, source_target_pairs={{68,64},{77,65},{70,66},{79,67},{64,68},{73,69},{66,70},{75,71},{7... | collective-permute-start | bytes 589832 | tf_op jit(solution)/shard_map/ppermute | solution.py:488
  93.2 1.9 %collective-permute-start.21 = (f32[48,1024]{1,0:T(8,128)S(1)}, f32[48,1024]{1,0:T(8,128)S(1)}, u32[]{:S(2)}, u32[]{:S(2)}) collective-permute-start(f32[48,1024]{1,0:T(8,128)S(1)} %collective-permute-done.17), channel_id=1, source_target_pairs={{76,64},{69,65},{78,66},{71,67},{72,68},{65,69},{74,70},{67,71},{6... | collective-permute-start | bytes 589832 | tf_op jit(solution)/shard_map/ppermute | solution.py:488
  96.2 3.0 %collective-permute-start.23 = (f32[48,1024]{1,0:T(8,128)S(1)}, f32[48,1024]{1,0:T(8,128)S(1)}, u32[]{:S(2)}, u32[]{:S(2)}) collective-permute-start(f32[48,1024]{1,0:T(8,128)S(1)} %collective-permute-done.19), channel_id=1, source_target_pairs={{76,64},{69,65},{78,66},{71,67},{72,68},{65,69},{74,70},{67,71},{6... | collective-permute-start | bytes 589832 | tf_op jit(solution)/shard_map/ppermute | solution.py:488
  99.5 1.4 collective-permute-start.15
  100.9 1.3 collective-permute-start.13
  102.2 2.6 %collective-permute-start.20 = (f32[48,1024]{1,0:T(8,128)S(1)}, f32[48,1024]{1,0:T(8,128)}, u32[]{:S(2)}, u32[]{:S(2)}) collective-permute-start(f32[48,1024]{1,0:T(8,128)S(1)} %collective-permute-done.19), channel_id=1, source_target_pairs={{0,1},{1,0},{2,3},{3,2},{4,5},{5,4},{6,7},{7,6},{8,9},{9,8},{10,11... | collective-permute-start | bytes 589832 | tf_op jit(solution)/shard_map/ppermute | solution.py:484
  107.5 1.3 collective-permute-start.25
  108.8 16.8 %collective-permute-done.25 = f32[48,1024]{1,0:T(8,128)} collective-permute-done((f32[48,1024]{1,0:T(8,128)}, f32[48,1024]{1,0:T(8,128)}, u32[]{:S(2)}, u32[]{:S(2)}) %collective-permute-start.25) | collective-permute-done | bytes 196640 | tf_op jit(solution)/shard_map/ppermute | solution.py:503
  126.6 1.4 %collective-permute-done.26 = f32[48,1024]{1,0:T(8,128)} collective-permute-done((f32[48,1024]{1,0:T(8,128)}, f32[48,1024]{1,0:T(8,128)}, u32[]{:S(2)}, u32[]{:S(2)}) %collective-permute-start.26) | collective-permute-done | bytes 196640 | tf_op jit(solution)/shard_map/ppermute | solution.py:484
  128.0 9.2 %conditional.9 = (f32[1,48,512]{2,1,0:T(8,128)}) conditional(s32[]{:T(128)} %convert_element_type.35, f32[48,512]{1,0:T(8,128)} %get-tuple-element.400, (s32[2]{0:T(128)S(1)}, s32[1]{0:T(128)}, f32[48,1024]{1,0:T(8,128)}, f32[48,1024]{1,0:T(8,128)}, f32[48,1024]{1,0:T(8,128)S(1)}, /*index=5*/f32[48,1024]{1,0:T(8,128)S(1)}, ...), branch_computations={%region_9.10_spmd, %region_10.11_spmd} | conditional | bytes 776 | solution.py:500
  128.2 9.0 %links_8_1.1 = (f32[48,1024]{1,0:T(8,128)}, f32[48,512]{1,0:T(8,128)}) custom-call(s32[2]{0:T(128)S(1)} %get-tuple-element.338.refs_0_, s32[1]{0:T(128)} %get-tuple-element.339.refs_1_, f32[48,1024]{1,0:T(8,128)} %get-tuple-element.340.refs_2_, f32[48,1024]{1,0:T(8,128)} %get-tuple-element.341.refs_3_, f32[48,1024]{1,0:T(8,128)S(1)} %get-tuple-element.342.refs_4_, ...), custom_call_target="tpu_custom_call" | custom-call | tf_op jit(solution)/shard_map/cond/branch_1_fun/links_8_1/pallas_call | solution.py:433
  (69 shorter events, 13.8 us)
Async XLA Ops:
  1.9 9.7 %collective-permute-start.1 = (f32[144,512]{1,0:T(8,128)S(1)}, f32[144,512]{1,0:T(8,128)S(1)}, u32[]{:S(2)}, u32[]{:S(2)}) collective-permute-start(f32[144,512]{1,0:T(8,128)S(1)} %constant_dynamic-update-slice_fusion.own), channel_id=1, source_target_pairs={{18,0},{3,1},{0,2},{17,3},{22,4},{7,5},{4,6},{21,7},{26,8},{11,9},... | collective-permute-start | bytes 884744 | tf_op jit(solution)/shard_map/ppermute | solution.py:466
  4.7 8.4 %collective-permute-start = (f32[144,512]{1,0:T(8,128)S(1)}, f32[144,512]{1,0:T(8,128)S(1)}, u32[]{:S(2)}, u32[]{:S(2)}) collective-permute-start(f32[144,512]{1,0:T(8,128)S(1)} %constant_dynamic-update-slice_fusion.own), channel_id=1, source_target_pairs={{0,1},{1,0},{2,3},{3,2},{4,5},{5,4},{6,7},{7,6},{8,9},{9,8},{10,11... | collective-permute-start | bytes 884744 | tf_op jit(solution)/shard_map/ppermute | solution.py:467
  54.4 9.8 %collective-permute-start.3 = (f32[48,1024]{1,0:T(8,128)S(1)}, f32[48,1024]{1,0:T(8,128)S(1)}, u32[]{:S(2)}, u32[]{:S(2)}) collective-permute-start(f32[48,1024]{1,0:T(8,128)S(1)} %get-tuple-element.399), channel_id=1, source_target_pairs={{20,16},{29,17},{22,18},{31,19},{16,20},{25,21},{18,22},{27,23},{2... | collective-permute-start | bytes 589832 | tf_op jit(solution)/shard_map/ppermute | solution.py:488
  61.1 8.5 %collective-permute-start.5 = (f32[48,1024]{1,0:T(8,128)S(1)}, f32[48,1024]{1,0:T(8,128)S(1)}, u32[]{:S(2)}, u32[]{:S(2)}) collective-permute-start(f32[48,1024]{1,0:T(8,128)S(1)} %get-tuple-element.399), channel_id=1, source_target_pairs={{28,16},{21,17},{30,18},{23,19},{24,20},{17,21},{26,22},{19,23},{2... | collective-permute-start | bytes 589832 | tf_op jit(solution)/shard_map/ppermute | solution.py:488
  64.2 6.7 %collective-permute-start.7 = (f32[48,1024]{1,0:T(8,128)S(1)}, f32[48,1024]{1,0:T(8,128)S(1)}, u32[]{:S(2)}, u32[]{:S(2)}) collective-permute-start(f32[48,1024]{1,0:T(8,128)S(1)} %collective-permute-done.3), channel_id=1, source_target_pairs={{28,16},{21,17},{30,18},{23,19},{24,20},{17,21},{26,22},{19,23},{2... | collective-permute-start | bytes 589832 | tf_op jit(solution)/shard_map/ppermute | solution.py:488
  66.4 6.8 %collective-permute-start.4 = (f32[48,1024]{1,0:T(8,128)S(1)}, f32[48,1024]{1,0:T(8,128)S(1)}, u32[]{:S(2)}, u32[]{:S(2)}) collective-permute-start(f32[48,1024]{1,0:T(8,128)S(1)} %collective-permute-done.3), channel_id=1, source_target_pairs={{0,1},{1,0},{2,3},{3,2},{4,5},{5,4},{6,7},{7,6},{8,9},{9,8},{10,11... | collective-permute-start | bytes 589832 | tf_op jit(solution)/shard_map/ppermute | solution.py:484
  69.6 3.6 %collective-permute-start.6 = (f32[48,1024]{1,0:T(8,128)S(1)}, f32[48,1024]{1,0:T(8,128)S(1)}, u32[]{:S(2)}, u32[]{:S(2)}) collective-permute-start(f32[48,1024]{1,0:T(8,128)S(1)} %collective-permute-done.5), channel_id=1, source_target_pairs={{0,1},{1,0},{2,3},{3,2},{4,5},{5,4},{6,7},{7,6},{8,9},{9,8},{10,11... | collective-permute-start | bytes 589832 | tf_op jit(solution)/shard_map/ppermute | solution.py:484
  70.9 3.4 %collective-permute-start.8 = (f32[48,1024]{1,0:T(8,128)S(1)}, f32[48,1024]{1,0:T(8,128)S(1)}, u32[]{:S(2)}, u32[]{:S(2)}) collective-permute-start(f32[48,1024]{1,0:T(8,128)S(1)} %collective-permute-done.7), channel_id=1, source_target_pairs={{0,1},{1,0},{2,3},{3,2},{4,5},{5,4},{6,7},{7,6},{8,9},{9,8},{10,11... | collective-permute-start | bytes 589832 | tf_op jit(solution)/shard_map/ppermute | solution.py:484
  75.0 8.1 %collective-permute-start.10 = (f32[48,1024]{1,0:T(8,128)S(1)}, f32[48,1024]{1,0:T(8,128)S(1)}, u32[]{:S(2)}, u32[]{:S(2)}) collective-permute-start(f32[48,1024]{1,0:T(8,128)S(1)} %collective-permute-done.9), channel_id=1, source_target_pairs={{0,1},{1,0},{2,3},{3,2},{4,5},{5,4},{6,7},{7,6},{8,9},{9,8},{10,11... | collective-permute-start | bytes 589832 | tf_op jit(solution)/shard_map/ppermute | solution.py:484
  75.4 12.8 %collective-permute-start.17 = (f32[48,1024]{1,0:T(8,128)S(1)}, f32[48,1024]{1,0:T(8,128)S(1)}, u32[]{:S(2)}, u32[]{:S(2)}) collective-permute-start(f32[48,1024]{1,0:T(8,128)S(1)} %get-tuple-element.399), channel_id=1, source_target_pairs={{80,64},{84,68},{88,72},{92,76},{64,80},{68,84},{72,88},{76,92},{1... | collective-permute-start | bytes 589832 | tf_op jit(solution)/shard_map/ppermute | solution.py:507
  83.1 9.9 %collective-permute-start.11 = (f32[48,1024]{1,0:T(8,128)S(1)}, f32[48,1024]{1,0:T(8,128)}, u32[]{:S(2)}, u32[]{:S(2)}) collective-permute-start(f32[48,1024]{1,0:T(8,128)S(1)} %get-tuple-element.397), channel_id=1, source_target_pairs={{32,48},{36,52},{40,56},{44,60},{33,49},{37,53},{41,57},{45,61},{3... | collective-permute-start | bytes 589832 | tf_op jit(solution)/shard_map/ppermute | solution.py:503
  88.2 8.0 %collective-permute-start.19 = (f32[48,1024]{1,0:T(8,128)S(1)}, f32[48,1024]{1,0:T(8,128)S(1)}, u32[]{:S(2)}, u32[]{:S(2)}) collective-permute-start(f32[48,1024]{1,0:T(8,128)S(1)} %collective-permute-done.17), channel_id=1, source_target_pairs={{68,64},{77,65},{70,66},{79,67},{64,68},{73,69},{66,70},{75,71},{7... | collective-permute-start | bytes 589832 | tf_op jit(solution)/shard_map/ppermute | solution.py:488
  93.1 6.2 %collective-permute-start.12 = (f32[48,1024]{1,0:T(8,128)}, f32[48,1024]{1,0:T(8,128)}, u32[]{:S(2)}, u32[]{:S(2)}) collective-permute-start(f32[48,1024]{1,0:T(8,128)} %collective-permute-done.11), channel_id=1, source_target_pairs={{0,1},{1,0},{2,3},{3,2},{4,5},{5,4},{6,7},{7,6},{8,9},{9,8},{10,11... | collective-permute-start | bytes 589832 | tf_op jit(solution)/shard_map/ppermute | solution.py:484
  93.2 9.0 %collective-permute-start.21 = (f32[48,1024]{1,0:T(8,128)S(1)}, f32[48,1024]{1,0:T(8,128)S(1)}, u32[]{:S(2)}, u32[]{:S(2)}) collective-permute-start(f32[48,1024]{1,0:T(8,128)S(1)} %collective-permute-done.17), channel_id=1, source_target_pairs={{76,64},{69,65},{78,66},{71,67},{72,68},{65,69},{74,70},{67,71},{6... | collective-permute-start | bytes 589832 | tf_op jit(solution)/shard_map/ppermute | solution.py:488
  95.1 9.7 %collective-permute-start.18 = (f32[48,1024]{1,0:T(8,128)S(1)}, f32[48,1024]{1,0:T(8,128)S(1)}, u32[]{:S(2)}, u32[]{:S(2)}) collective-permute-start(f32[48,1024]{1,0:T(8,128)S(1)} %collective-permute-done.17), channel_id=1, source_target_pairs={{0,1},{1,0},{2,3},{3,2},{4,5},{5,4},{6,7},{7,6},{8,9},{9,8},{10,11... | collective-permute-start | bytes 589832 | tf_op jit(solution)/shard_map/ppermute | solution.py:484
  96.2 8.7 %collective-permute-start.23 = (f32[48,1024]{1,0:T(8,128)S(1)}, f32[48,1024]{1,0:T(8,128)S(1)}, u32[]{:S(2)}, u32[]{:S(2)}) collective-permute-start(f32[48,1024]{1,0:T(8,128)S(1)} %collective-permute-done.19), channel_id=1, source_target_pairs={{76,64},{69,65},{78,66},{71,67},{72,68},{65,69},{74,70},{67,71},{6... | collective-permute-start | bytes 589832 | tf_op jit(solution)/shard_map/ppermute | solution.py:488
  99.5 6.0 %collective-permute-start.15 = (f32[48,1024]{1,0:T(8,128)}, f32[48,1024]{1,0:T(8,128)}, u32[]{:S(2)}, u32[]{:S(2)}) collective-permute-start(f32[48,1024]{1,0:T(8,128)} %get-tuple-element.398), channel_id=1, source_target_pairs={{48,80},{52,84},{56,88},{60,92},{49,81},{53,85},{57,89},{61,93},{5... | collective-permute-start | bytes 589832 | tf_op jit(solution)/shard_map/ppermute | solution.py:503
  100.9 4.6 %collective-permute-start.13 = (f32[48,1024]{1,0:T(8,128)}, f32[48,1024]{1,0:T(8,128)}, u32[]{:S(2)}, u32[]{:S(2)}) collective-permute-start(f32[48,1024]{1,0:T(8,128)} %get-tuple-element.398), channel_id=1, source_target_pairs={{48,64},{52,68},{56,72},{60,76},{49,65},{53,69},{57,73},{61,77},{5... | collective-permute-start | bytes 589832 | tf_op jit(solution)/shard_map/ppermute | solution.py:503
  102.2 4.2 %collective-permute-start.20 = (f32[48,1024]{1,0:T(8,128)S(1)}, f32[48,1024]{1,0:T(8,128)}, u32[]{:S(2)}, u32[]{:S(2)}) collective-permute-start(f32[48,1024]{1,0:T(8,128)S(1)} %collective-permute-done.19), channel_id=1, source_target_pairs={{0,1},{1,0},{2,3},{3,2},{4,5},{5,4},{6,7},{7,6},{8,9},{9,8},{10,11... | collective-permute-start | bytes 589832 | tf_op jit(solution)/shard_map/ppermute | solution.py:484
  104.9 2.0 %collective-permute-start.24 = (f32[48,1024]{1,0:T(8,128)S(1)}, f32[48,1024]{1,0:T(8,128)}, u32[]{:S(2)}, u32[]{:S(2)}) collective-permute-start(f32[48,1024]{1,0:T(8,128)S(1)} %collective-permute-done.23), channel_id=1, source_target_pairs={{0,1},{1,0},{2,3},{3,2},{4,5},{5,4},{6,7},{7,6},{8,9},{9,8},{10,11... | collective-permute-start | bytes 589832 | tf_op jit(solution)/shard_map/ppermute | solution.py:484
  105.5 1.8 %collective-permute-start.16 = (f32[48,1024]{1,0:T(8,128)}, f32[48,1024]{1,0:T(8,128)}, u32[]{:S(2)}, u32[]{:S(2)}) collective-permute-start(f32[48,1024]{1,0:T(8,128)} %collective-permute-done.15), channel_id=1, source_target_pairs={{0,1},{1,0},{2,3},{3,2},{4,5},{5,4},{6,7},{7,6},{8,9},{9,8},{10,11... | collective-permute-start | bytes 589832 | tf_op jit(solution)/shard_map/ppermute | solution.py:484
  105.5 2.1 %collective-permute-start.14 = (f32[48,1024]{1,0:T(8,128)}, f32[48,1024]{1,0:T(8,128)}, u32[]{:S(2)}, u32[]{:S(2)}) collective-permute-start(f32[48,1024]{1,0:T(8,128)} %collective-permute-done.13), channel_id=1, source_target_pairs={{0,1},{1,0},{2,3},{3,2},{4,5},{5,4},{6,7},{7,6},{8,9},{9,8},{10,11... | collective-permute-start | bytes 589832 | tf_op jit(solution)/shard_map/ppermute | solution.py:484
  107.5 18.1 %collective-permute-start.25 = (f32[48,1024]{1,0:T(8,128)}, f32[48,1024]{1,0:T(8,128)}, u32[]{:S(2)}, u32[]{:S(2)}) collective-permute-start(f32[48,1024]{1,0:T(8,128)} %get-tuple-element.401), channel_id=1, source_target_pairs={{64,96},{68,100},{72,104},{76,108},{80,112},{84,116},{88,120},{92,... | collective-permute-start | bytes 589832 | tf_op jit(solution)/shard_map/ppermute | solution.py:503
  125.7 2.3 %collective-permute-start.26 = (f32[48,1024]{1,0:T(8,128)}, f32[48,1024]{1,0:T(8,128)}, u32[]{:S(2)}, u32[]{:S(2)}) collective-permute-start(f32[48,1024]{1,0:T(8,128)} %collective-permute-done.25), channel_id=1, source_target_pairs={{0,1},{1,0},{2,3},{3,2},{4,5},{5,4},{6,7},{7,6},{8,9},{9,8},{10,11... | collective-permute-start | bytes 589832 | tf_op jit(solution)/shard_map/ppermute | solution.py:484
  (10 other events, 20.8 us)
